TPU v7x, 128 devices: a whole 4x4x4 slice. The times are simulated.
128 devices in a mesh: hst: 32 (over z, y, core), local: 4 (over x).
Axes of the slice: x: 4, y: 4, z: 4, core: 2. Of those that a mesh axis runs over, the one named last changes fastest.
Arguments:
- features: bfloat16 [16384, 3456], P(('hst', 'local')), may hold values from -6 to 6
- labels: int32 [16384], P(('hst', 'local')), may hold values 0 or 1
- cross_down: bfloat16 [512, 3456], replicated, may hold values from -0.109375 to 0.109375
- cross_up: bfloat16 [512, 3456], replicated, may hold values from -0.25 to 0.25
- cross_bias: float32 [3456], replicated, may hold values from -2 to 2
- head_weight: float32 [3456], replicated, may hold values from -0.109375 to 0.109375
- head_bias: float32 [1], replicated, may hold values from -2 to 2
- table_place: int32 [22], replicated, may hold values from 0 to 31, as said below
- bag_rows: int32 [16384, 22, 4], P(('hst', 'local')), may hold values from 0 to 16383
- small_rows: int32 [16384, 4, 4], P(('hst', 'local')), may hold values from 0 to 1023
- table_store: float32 [524288, 128], P(('hst', 'local')), may hold values from -0.6 to 0.6
- table_acc: float32 [524288], P(('hst', 'local')), may hold values from 0.01 to 1
- small_store: float32 [4096, 128], replicated, may hold values from -0.6 to 0.6
- small_acc: float32 [4096], replicated, may hold values from 0.001 to 0.1
- down_acc: float32 [512, 3456], P(('hst', 'local')), may hold values from 1 to 100
- up_acc: float32 [512, 3456], P(('hst', 'local')), may hold values from 1 to 100
Outputs:
- table_new: float32 [524288, 128], P(('hst', 'local'))
- table_acc_new: float32 [524288], P(('hst', 'local'))
- small_new: float32 [4096, 128], replicated
- small_acc_new: float32 [4096], replicated
- down_step: float32 [512, 3456], P(('hst', 'local'))
- up_step: float32 [512, 3456], P(('hst', 'local'))
Inputs may be any that keep to these rules, and one draw needn't show every extreme that they name: `table_place`: the 22 values are distinct, so no two tables share a slot; the last slot of the last host is always used.
All inputs are finite; a program needn't handle non-finite values. No bound on the sum of `labels` on one device may be relied on, other than what follows from the above.
Results may differ from a plain program's by a relative error of at most 0.0047.
Values sent between devices are 32-bit elements; how exact they have to be, the bound alone decides.
A program may use at most 128 MiB of HBM per device.

v0:
```python
import math

import jax
import jax.numpy as jnp
from jax import lax
from jax.sharding import PartitionSpec as P

TS = 22
TR = 4
RS = 1024
HOT = 4
SHARD = 4096


LEARN_RATE = 0.05


def dense_backward(
    block_features, block_labels, cross_down, cross_up, cross_bias, head_weight, head_bias
):
    low_proj = lax.dot_general(
        block_features, cross_down, (((1,), (1,)), ((), ())), preferred_element_type=jnp.float32
    ).astype(jnp.bfloat16)
    cross_out = jnp.dot(low_proj, cross_up, preferred_element_type=jnp.float32) + cross_bias
    wide_input = block_features.astype(jnp.float32)
    layer_out = wide_input * cross_out + wide_input
    logit = jnp.dot(layer_out, head_weight, precision=lax.Precision.HIGHEST) + head_bias[0]
    logit_grad = jax.nn.sigmoid(logit) - block_labels.astype(jnp.float32)
    layer_grad = logit_grad[:, None] * head_weight[None, :]
    cross_grad = (layer_grad * wide_input).astype(jnp.bfloat16)
    low_grad = lax.dot_general(
        cross_grad, cross_up, (((1,), (1,)), ((), ())), preferred_element_type=jnp.float32
    ).astype(jnp.bfloat16)
    feature_grad = layer_grad * (cross_out + 1.0) + jnp.dot(
        low_grad, cross_down, preferred_element_type=jnp.float32
    )
    return (feature_grad, low_proj, cross_grad, low_grad)


def rowwise_adagrad(stored, accum, grads):
    accum_new = accum + jnp.mean(grads * grads, axis=1)
    return (stored - LEARN_RATE * grads / jnp.sqrt(accum_new)[:, None], accum_new)


def pooled_rows(row_ids, grads, row_total):
    block = math.gcd(row_total, 512)
    block_count = row_total // block

    def one_block(block_index):
        wanted = block_index * block + jnp.arange(block, dtype=jnp.int32)
        counts = jnp.zeros((block, row_ids.shape[0]), jnp.float32)
        for pooled in range(row_ids.shape[1]):
            counts = counts + (row_ids[None, :, pooled] == wanted[:, None]).astype(jnp.float32)
        return jnp.dot(counts, grads, precision=lax.Precision.HIGHEST)

    blocks = lax.map(one_block, jnp.arange(block_count, dtype=jnp.int32))
    return blocks.reshape(row_total, grads.shape[1])


def on_device(
    features,
    labels,
    cross_down,
    cross_up,
    cross_bias,
    head_weight,
    head_bias,
    table_place,
    bag_rows,
    small_rows,
    table_store,
    table_acc,
    small_store,
    small_acc,
    down_acc,
    up_acc,
):
    n_hosts = lax.axis_size("hst")
    n_locals = lax.axis_size("local")
    sample_count = features.shape[0]
    emb_width = table_store.shape[1]
    dev_rows = table_store.shape[0]
    slots_host = dev_rows // SHARD
    slot_total = n_hosts * slots_host
    feature_grad, low_proj, cross_grad, low_grad = dense_backward(
        features, labels, cross_down, cross_up, cross_bias, head_weight, head_bias
    )
    bag_grads = feature_grad[:, emb_width : emb_width * (1 + TS)].reshape(
        sample_count, TS, emb_width
    )
    slot_of = table_place % slots_host
    host_ids = bag_rows // SHARD * dev_rows + slot_of[None, :, None] * SHARD + bag_rows % SHARD
    placing = table_place[None, :] == jnp.arange(slot_total, dtype=jnp.int32)[:, None]
    send_grads = jnp.einsum(
        "st,bte->sbe", placing.astype(jnp.float32), bag_grads, precision=lax.Precision.HIGHEST
    )
    send_ids = jnp.sum(
        jnp.where(placing[:, :, None, None], jnp.transpose(host_ids, (1, 0, 2))[None], 0), axis=1
    )
    got_grads, got_ids = (
        lax.all_to_all(send_grads, "hst", split_axis=0, concat_axis=0, tiled=True),
        lax.all_to_all(send_ids, "hst", split_axis=0, concat_axis=0, tiled=True),
    )
    got_grads = got_grads.reshape(-1, emb_width)
    got_ids = got_ids.reshape(-1, HOT)
    host_grad = pooled_rows(got_ids, got_grads, n_locals * dev_rows)
    table_grad = lax.psum_scatter(host_grad, "local", scatter_dimension=0, tiled=True)
    table_new, table_acc_new = rowwise_adagrad(table_store, table_acc, table_grad)
    part = low_grad
    down_grad = lax.psum_scatter(
        lax.dot_general(
            part, features, (((0,), (0,)), ((), ())), preferred_element_type=jnp.float32
        ),
        ("hst", "local"),
        scatter_dimension=0,
        tiled=True,
    )
    part = low_proj
    up_grad = lax.psum_scatter(
        lax.dot_general(
            part, cross_grad, (((0,), (0,)), ((), ())), preferred_element_type=jnp.float32
        ),
        ("hst", "local"),
        scatter_dimension=0,
        tiled=True,
    )
    down_step = down_grad / jnp.sqrt(down_acc + down_grad * down_grad)
    up_step = up_grad / jnp.sqrt(up_acc + up_grad * up_grad)
    small_grads = feature_grad[:, emb_width * (1 + TS) :].reshape(sample_count, TR, emb_width)
    small_local = jnp.concatenate(
        [pooled_rows(small_rows[:, table, :], small_grads[:, table, :], RS) for table in range(TR)],
        axis=0,
    )
    small_total = lax.psum(small_local, ("hst", "local"))
    small_new, small_acc_new = rowwise_adagrad(small_store, small_acc, small_total)
    return (table_new, table_acc_new, small_new, small_acc_new, down_step, up_step)


def solution(mesh):
    placed = (
        P(("hst", "local"), None),
        P(("hst", "local")),
        P(),
        P(),
        P(),
        P(),
        P(),
        P(),
        P(("hst", "local"), None, None),
        P(("hst", "local"), None, None),
        P(("hst", "local"), None),
        P(("hst", "local")),
        P(),
        P(),
        P(("hst", "local"), None),
        P(("hst", "local"), None),
    )
    return jax.shard_map(
        on_device,
        mesh=mesh,
        in_specs=placed,
        out_specs=(
            P(("hst", "local"), None),
            P(("hst", "local")),
            P(),
            P(),
            P(("hst", "local"), None),
            P(("hst", "local"), None),
        ),
        check_vma=False,
    )
```

profile of v0, /device:TPU:0, one launch (start us, length us, event | category | flops | bytes accessed | tf_op | source)
XLA Modules:
  0.0 572.9 jit_solution(14851624625134548136)
XLA Ops:
  10.7 8.5 %all-to-all-start = ((s32[32,128,4]{1,2,0:T(4,128)}), s32[32,128,4]{1,2,0:T(4,128)}, u32[]{:S(2)}, u32[]{:S(2)}) async-start(s32[32,128,4]{1,2,0:T(4,128)} %copy.46), calls=%async_computation | async-start | bytes 131072 | tf_op jit(solution)/shard_map/all_to_all | solution.py:102
  20.6 3.5 convolution_convert_fusion.1
  25.3 1.6 fusion.99
  27.0 1.3 convolution_convert_fusion
  28.3 4.1 fusion.100
  34.2 3.5 while.51
  37.8 3.5 while.52
  42.3 4.9 while.53
  43.6 1.2 fusion.160
  46.0 1.2 fusion.160
  47.7 1.6 copy.48
  49.3 2.5 fusion.108
  51.8 2.5 copy.49
  54.3 7.5 %all-to-all-start.1 = ((f32[32,128,128]{2,1,0:T(8,128)}), f32[32,128,128]{2,1,0:T(8,128)S(1)}, u32[]{:S(2)}, u32[]{:S(2)}) async-start(f32[32,128,128]{2,1,0:T(8,128)} %copy.49), calls=%async_computation.1 | async-start | bytes 4194304 | tf_op jit(solution)/shard_map/all_to_all | solution.py:101
  61.9 4.0 fusion.114
  65.9 5.2 while.54
  67.2 1.3 fusion.163
  69.8 1.3 fusion.163
  71.1 2.7 pad_maximum_fusion
  74.0 18.6 %all-to-all-done.1 = f32[32,128,128]{2,1,0:T(8,128)S(1)} async-done(((f32[32,128,128]{2,1,0:T(8,128)}), f32[32,128,128]{2,1,0:T(8,128)S(1)}, u32[]{:S(2)}, u32[]{:S(2)}) %all-to-all-start.1) | async-done | bytes 2097184 | tf_op jit(solution)/shard_map/all_to_all | solution.py:101
  92.6 388.8 %while.50 = (s32[]{:T(128)}, f32[32,512,128]{2,1,0:T(8,128)}, s32[4096,4]{0,1:T(4,128)}, s32[32]{0:T(128)S(1)}, f32[4096,128]{1,0:T(8,128)S(1)}, /*index=5*/s32[]{:T(128)}, s32[1]{0:T(128)}) while((s32[]{:T(128)}, f32[32,512,128]{2,1,0:T(8,128)}, s32[4096,4]{0,1:T(4,128)}, s32[32]{0:T(128)S(1)}, f32[4096,128]{1,0:T(8,128)S(1)}, ...), condition=%wide.region_2.3_spmd, body=%wide.region_1.2_spmd.sunk | while | flops 3244294656 | bytes 2560617 | solution.py:56
  92.6 1.1 fusion.150
  94.9 9.8 %fusion.151 = f32[32,512,128]{2,1,0:T(8,128)} fusion(f32[32,512,128]{2,1,0:T(8,128)} %get-tuple-element.436, s32[]{:T(128)} %get-tuple-element.435, f32[4096,128]{1,0:T(8,128)S(1)} %get-tuple-element.446, s32[4096]{0:T(1024)S(1)} %bitcast.180, s32[4096]{0:T(1024)S(1)} %bitcast.181, s32[4096]{0:T(1024)S(1)} %bitcast.182, s32[4096]{0:T(1024)S(1)} %bitcast.179, ...), kind=kOutput, calls=%fused_computation.18.clone.1 | convolution fusion | flops 3244294144 | bytes 2427392 | tf_op jit(solution)/shard_map/while/body/eval_jaxpr/dot_general | solution.py:54
  104.7 1.1 fusion.150
  107.0 9.8 %fusion.151 = f32[32,512,128]{2,1,0:T(8,128)} fusion(f32[32,512,128]{2,1,0:T(8,128)} %get-tuple-element.436, s32[]{:T(128)} %get-tuple-element.435, f32[4096,128]{1,0:T(8,128)S(1)} %get-tuple-element.446, s32[4096]{0:T(1024)S(1)} %bitcast.180, s32[4096]{0:T(1024)S(1)} %bitcast.181, s32[4096]{0:T(1024)S(1)} %bitcast.182, s32[4096]{0:T(1024)S(1)} %bitcast.179, ...), kind=kOutput, calls=%fused_computation.18.clone.1 | convolution fusion | flops 3244294144 | bytes 2427392 | tf_op jit(solution)/shard_map/while/body/eval_jaxpr/dot_general | solution.py:54
  116.9 1.1 fusion.150
  119.2 9.8 %fusion.151 = f32[32,512,128]{2,1,0:T(8,128)} fusion(f32[32,512,128]{2,1,0:T(8,128)} %get-tuple-element.436, s32[]{:T(128)} %get-tuple-element.435, f32[4096,128]{1,0:T(8,128)S(1)} %get-tuple-element.446, s32[4096]{0:T(1024)S(1)} %bitcast.180, s32[4096]{0:T(1024)S(1)} %bitcast.181, s32[4096]{0:T(1024)S(1)} %bitcast.182, s32[4096]{0:T(1024)S(1)} %bitcast.179, ...), kind=kOutput, calls=%fused_computation.18.clone.1 | convolution fusion | flops 3244294144 | bytes 2427392 | tf_op jit(solution)/shard_map/while/body/eval_jaxpr/dot_general | solution.py:54
  129.0 1.1 fusion.150
  131.3 9.8 %fusion.151 = f32[32,512,128]{2,1,0:T(8,128)} fusion(f32[32,512,128]{2,1,0:T(8,128)} %get-tuple-element.436, s32[]{:T(128)} %get-tuple-element.435, f32[4096,128]{1,0:T(8,128)S(1)} %get-tuple-element.446, s32[4096]{0:T(1024)S(1)} %bitcast.180, s32[4096]{0:T(1024)S(1)} %bitcast.181, s32[4096]{0:T(1024)S(1)} %bitcast.182, s32[4096]{0:T(1024)S(1)} %bitcast.179, ...), kind=kOutput, calls=%fused_computation.18.clone.1 | convolution fusion | flops 3244294144 | bytes 2427392 | tf_op jit(solution)/shard_map/while/body/eval_jaxpr/dot_general | solution.py:54
  143.5 9.8 %fusion.151 = f32[32,512,128]{2,1,0:T(8,128)} fusion(f32[32,512,128]{2,1,0:T(8,128)} %get-tuple-element.436, s32[]{:T(128)} %get-tuple-element.435, f32[4096,128]{1,0:T(8,128)S(1)} %get-tuple-element.446, s32[4096]{0:T(1024)S(1)} %bitcast.180, s32[4096]{0:T(1024)S(1)} %bitcast.181, s32[4096]{0:T(1024)S(1)} %bitcast.182, s32[4096]{0:T(1024)S(1)} %bitcast.179, ...), kind=kOutput, calls=%fused_computation.18.clone.1 | convolution fusion | flops 3244294144 | bytes 2427392 | tf_op jit(solution)/shard_map/while/body/eval_jaxpr/dot_general | solution.py:54
  155.6 9.8 %fusion.151 = f32[32,512,128]{2,1,0:T(8,128)} fusion(f32[32,512,128]{2,1,0:T(8,128)} %get-tuple-element.436, s32[]{:T(128)} %get-tuple-element.435, f32[4096,128]{1,0:T(8,128)S(1)} %get-tuple-element.446, s32[4096]{0:T(1024)S(1)} %bitcast.180, s32[4096]{0:T(1024)S(1)} %bitcast.181, s32[4096]{0:T(1024)S(1)} %bitcast.182, s32[4096]{0:T(1024)S(1)} %bitcast.179, ...), kind=kOutput, calls=%fused_computation.18.clone.1 | convolution fusion | flops 3244294144 | bytes 2427392 | tf_op jit(solution)/shard_map/while/body/eval_jaxpr/dot_general | solution.py:54
  167.8 9.9 %fusion.151 = f32[32,512,128]{2,1,0:T(8,128)} fusion(f32[32,512,128]{2,1,0:T(8,128)} %get-tuple-element.436, s32[]{:T(128)} %get-tuple-element.435, f32[4096,128]{1,0:T(8,128)S(1)} %get-tuple-element.446, s32[4096]{0:T(1024)S(1)} %bitcast.180, s32[4096]{0:T(1024)S(1)} %bitcast.181, s32[4096]{0:T(1024)S(1)} %bitcast.182, s32[4096]{0:T(1024)S(1)} %bitcast.179, ...), kind=kOutput, calls=%fused_computation.18.clone.1 | convolution fusion | flops 3244294144 | bytes 2427392 | tf_op jit(solution)/shard_map/while/body/eval_jaxpr/dot_general | solution.py:54
  179.9 9.8 %fusion.151 = f32[32,512,128]{2,1,0:T(8,128)} fusion(f32[32,512,128]{2,1,0:T(8,128)} %get-tuple-element.436, s32[]{:T(128)} %get-tuple-element.435, f32[4096,128]{1,0:T(8,128)S(1)} %get-tuple-element.446, s32[4096]{0:T(1024)S(1)} %bitcast.180, s32[4096]{0:T(1024)S(1)} %bitcast.181, s32[4096]{0:T(1024)S(1)} %bitcast.182, s32[4096]{0:T(1024)S(1)} %bitcast.179, ...), kind=kOutput, calls=%fused_computation.18.clone.1 | convolution fusion | flops 3244294144 | bytes 2427392 | tf_op jit(solution)/shard_map/while/body/eval_jaxpr/dot_general | solution.py:54
  192.1 9.8 %fusion.151 = f32[32,512,128]{2,1,0:T(8,128)} fusion(f32[32,512,128]{2,1,0:T(8,128)} %get-tuple-element.436, s32[]{:T(128)} %get-tuple-element.435, f32[4096,128]{1,0:T(8,128)S(1)} %get-tuple-element.446, s32[4096]{0:T(1024)S(1)} %bitcast.180, s32[4096]{0:T(1024)S(1)} %bitcast.181, s32[4096]{0:T(1024)S(1)} %bitcast.182, s32[4096]{0:T(1024)S(1)} %bitcast.179, ...), kind=kOutput, calls=%fused_computation.18.clone.1 | convolution fusion | flops 3244294144 | bytes 2427392 | tf_op jit(solution)/shard_map/while/body/eval_jaxpr/dot_general | solution.py:54
  204.2 9.9 %fusion.151 = f32[32,512,128]{2,1,0:T(8,128)} fusion(f32[32,512,128]{2,1,0:T(8,128)} %get-tuple-element.436, s32[]{:T(128)} %get-tuple-element.435, f32[4096,128]{1,0:T(8,128)S(1)} %get-tuple-element.446, s32[4096]{0:T(1024)S(1)} %bitcast.180, s32[4096]{0:T(1024)S(1)} %bitcast.181, s32[4096]{0:T(1024)S(1)} %bitcast.182, s32[4096]{0:T(1024)S(1)} %bitcast.179, ...), kind=kOutput, calls=%fused_computation.18.clone.1 | convolution fusion | flops 3244294144 | bytes 2427392 | tf_op jit(solution)/shard_map/while/body/eval_jaxpr/dot_general | solution.py:54
  214.1 1.1 fusion.150
  216.4 9.8 %fusion.151 = f32[32,512,128]{2,1,0:T(8,128)} fusion(f32[32,512,128]{2,1,0:T(8,128)} %get-tuple-element.436, s32[]{:T(128)} %get-tuple-element.435, f32[4096,128]{1,0:T(8,128)S(1)} %get-tuple-element.446, s32[4096]{0:T(1024)S(1)} %bitcast.180, s32[4096]{0:T(1024)S(1)} %bitcast.181, s32[4096]{0:T(1024)S(1)} %bitcast.182, s32[4096]{0:T(1024)S(1)} %bitcast.179, ...), kind=kOutput, calls=%fused_computation.18.clone.1 | convolution fusion | flops 3244294144 | bytes 2427392 | tf_op jit(solution)/shard_map/while/body/eval_jaxpr/dot_general | solution.py:54
  228.6 9.8 %fusion.151 = f32[32,512,128]{2,1,0:T(8,128)} fusion(f32[32,512,128]{2,1,0:T(8,128)} %get-tuple-element.436, s32[]{:T(128)} %get-tuple-element.435, f32[4096,128]{1,0:T(8,128)S(1)} %get-tuple-element.446, s32[4096]{0:T(1024)S(1)} %bitcast.180, s32[4096]{0:T(1024)S(1)} %bitcast.181, s32[4096]{0:T(1024)S(1)} %bitcast.182, s32[4096]{0:T(1024)S(1)} %bitcast.179, ...), kind=kOutput, calls=%fused_computation.18.clone.1 | convolution fusion | flops 3244294144 | bytes 2427392 | tf_op jit(solution)/shard_map/while/body/eval_jaxpr/dot_general | solution.py:54
  240.7 9.8 %fusion.151 = f32[32,512,128]{2,1,0:T(8,128)} fusion(f32[32,512,128]{2,1,0:T(8,128)} %get-tuple-element.436, s32[]{:T(128)} %get-tuple-element.435, f32[4096,128]{1,0:T(8,128)S(1)} %get-tuple-element.446, s32[4096]{0:T(1024)S(1)} %bitcast.180, s32[4096]{0:T(1024)S(1)} %bitcast.181, s32[4096]{0:T(1024)S(1)} %bitcast.182, s32[4096]{0:T(1024)S(1)} %bitcast.179, ...), kind=kOutput, calls=%fused_computation.18.clone.1 | convolution fusion | flops 3244294144 | bytes 2427392 | tf_op jit(solution)/shard_map/while/body/eval_jaxpr/dot_general | solution.py:54
  252.8 9.8 %fusion.151 = f32[32,512,128]{2,1,0:T(8,128)} fusion(f32[32,512,128]{2,1,0:T(8,128)} %get-tuple-element.436, s32[]{:T(128)} %get-tuple-element.435, f32[4096,128]{1,0:T(8,128)S(1)} %get-tuple-element.446, s32[4096]{0:T(1024)S(1)} %bitcast.180, s32[4096]{0:T(1024)S(1)} %bitcast.181, s32[4096]{0:T(1024)S(1)} %bitcast.182, s32[4096]{0:T(1024)S(1)} %bitcast.179, ...), kind=kOutput, calls=%fused_computation.18.clone.1 | convolution fusion | flops 3244294144 | bytes 2427392 | tf_op jit(solution)/shard_map/while/body/eval_jaxpr/dot_general | solution.py:54
  265.0 9.8 %fusion.151 = f32[32,512,128]{2,1,0:T(8,128)} fusion(f32[32,512,128]{2,1,0:T(8,128)} %get-tuple-element.436, s32[]{:T(128)} %get-tuple-element.435, f32[4096,128]{1,0:T(8,128)S(1)} %get-tuple-element.446, s32[4096]{0:T(1024)S(1)} %bitcast.180, s32[4096]{0:T(1024)S(1)} %bitcast.181, s32[4096]{0:T(1024)S(1)} %bitcast.182, s32[4096]{0:T(1024)S(1)} %bitcast.179, ...), kind=kOutput, calls=%fused_computation.18.clone.1 | convolution fusion | flops 3244294144 | bytes 2427392 | tf_op jit(solution)/shard_map/while/body/eval_jaxpr/dot_general | solution.py:54
  277.1 9.8 %fusion.151 = f32[32,512,128]{2,1,0:T(8,128)} fusion(f32[32,512,128]{2,1,0:T(8,128)} %get-tuple-element.436, s32[]{:T(128)} %get-tuple-element.435, f32[4096,128]{1,0:T(8,128)S(1)} %get-tuple-element.446, s32[4096]{0:T(1024)S(1)} %bitcast.180, s32[4096]{0:T(1024)S(1)} %bitcast.181, s32[4096]{0:T(1024)S(1)} %bitcast.182, s32[4096]{0:T(1024)S(1)} %bitcast.179, ...), kind=kOutput, calls=%fused_computation.18.clone.1 | convolution fusion | flops 3244294144 | bytes 2427392 | tf_op jit(solution)/shard_map/while/body/eval_jaxpr/dot_general | solution.py:54
  289.3 9.8 %fusion.151 = f32[32,512,128]{2,1,0:T(8,128)} fusion(f32[32,512,128]{2,1,0:T(8,128)} %get-tuple-element.436, s32[]{:T(128)} %get-tuple-element.435, f32[4096,128]{1,0:T(8,128)S(1)} %get-tuple-element.446, s32[4096]{0:T(1024)S(1)} %bitcast.180, s32[4096]{0:T(1024)S(1)} %bitcast.181, s32[4096]{0:T(1024)S(1)} %bitcast.182, s32[4096]{0:T(1024)S(1)} %bitcast.179, ...), kind=kOutput, calls=%fused_computation.18.clone.1 | convolution fusion | flops 3244294144 | bytes 2427392 | tf_op jit(solution)/shard_map/while/body/eval_jaxpr/dot_general | solution.py:54
  301.4 9.8 %fusion.151 = f32[32,512,128]{2,1,0:T(8,128)} fusion(f32[32,512,128]{2,1,0:T(8,128)} %get-tuple-element.436, s32[]{:T(128)} %get-tuple-element.435, f32[4096,128]{1,0:T(8,128)S(1)} %get-tuple-element.446, s32[4096]{0:T(1024)S(1)} %bitcast.180, s32[4096]{0:T(1024)S(1)} %bitcast.181, s32[4096]{0:T(1024)S(1)} %bitcast.182, s32[4096]{0:T(1024)S(1)} %bitcast.179, ...), kind=kOutput, calls=%fused_computation.18.clone.1 | convolution fusion | flops 3244294144 | bytes 2427392 | tf_op jit(solution)/shard_map/while/body/eval_jaxpr/dot_general | solution.py:54
  313.5 9.8 %fusion.151 = f32[32,512,128]{2,1,0:T(8,128)} fusion(f32[32,512,128]{2,1,0:T(8,128)} %get-tuple-element.436, s32[]{:T(128)} %get-tuple-element.435, f32[4096,128]{1,0:T(8,128)S(1)} %get-tuple-element.446, s32[4096]{0:T(1024)S(1)} %bitcast.180, s32[4096]{0:T(1024)S(1)} %bitcast.181, s32[4096]{0:T(1024)S(1)} %bitcast.182, s32[4096]{0:T(1024)S(1)} %bitcast.179, ...), kind=kOutput, calls=%fused_computation.18.clone.1 | convolution fusion | flops 3244294144 | bytes 2427392 | tf_op jit(solution)/shard_map/while/body/eval_jaxpr/dot_general | solution.py:54
  325.7 9.9 %fusion.151 = f32[32,512,128]{2,1,0:T(8,128)} fusion(f32[32,512,128]{2,1,0:T(8,128)} %get-tuple-element.436, s32[]{:T(128)} %get-tuple-element.435, f32[4096,128]{1,0:T(8,128)S(1)} %get-tuple-element.446, s32[4096]{0:T(1024)S(1)} %bitcast.180, s32[4096]{0:T(1024)S(1)} %bitcast.181, s32[4096]{0:T(1024)S(1)} %bitcast.182, s32[4096]{0:T(1024)S(1)} %bitcast.179, ...), kind=kOutput, calls=%fused_computation.18.clone.1 | convolution fusion | flops 3244294144 | bytes 2427392 | tf_op jit(solution)/shard_map/while/body/eval_jaxpr/dot_general | solution.py:54
  337.9 9.8 %fusion.151 = f32[32,512,128]{2,1,0:T(8,128)} fusion(f32[32,512,128]{2,1,0:T(8,128)} %get-tuple-element.436, s32[]{:T(128)} %get-tuple-element.435, f32[4096,128]{1,0:T(8,128)S(1)} %get-tuple-element.446, s32[4096]{0:T(1024)S(1)} %bitcast.180, s32[4096]{0:T(1024)S(1)} %bitcast.181, s32[4096]{0:T(1024)S(1)} %bitcast.182, s32[4096]{0:T(1024)S(1)} %bitcast.179, ...), kind=kOutput, calls=%fused_computation.18.clone.1 | convolution fusion | flops 3244294144 | bytes 2427392 | tf_op jit(solution)/shard_map/while/body/eval_jaxpr/dot_general | solution.py:54
  350.0 9.8 %fusion.151 = f32[32,512,128]{2,1,0:T(8,128)} fusion(f32[32,512,128]{2,1,0:T(8,128)} %get-tuple-element.436, s32[]{:T(128)} %get-tuple-element.435, f32[4096,128]{1,0:T(8,128)S(1)} %get-tuple-element.446, s32[4096]{0:T(1024)S(1)} %bitcast.180, s32[4096]{0:T(1024)S(1)} %bitcast.181, s32[4096]{0:T(1024)S(1)} %bitcast.182, s32[4096]{0:T(1024)S(1)} %bitcast.179, ...), kind=kOutput, calls=%fused_computation.18.clone.1 | convolution fusion | flops 3244294144 | bytes 2427392 | tf_op jit(solution)/shard_map/while/body/eval_jaxpr/dot_general | solution.py:54
  362.2 9.8 %fusion.151 = f32[32,512,128]{2,1,0:T(8,128)} fusion(f32[32,512,128]{2,1,0:T(8,128)} %get-tuple-element.436, s32[]{:T(128)} %get-tuple-element.435, f32[4096,128]{1,0:T(8,128)S(1)} %get-tuple-element.446, s32[4096]{0:T(1024)S(1)} %bitcast.180, s32[4096]{0:T(1024)S(1)} %bitcast.181, s32[4096]{0:T(1024)S(1)} %bitcast.182, s32[4096]{0:T(1024)S(1)} %bitcast.179, ...), kind=kOutput, calls=%fused_computation.18.clone.1 | convolution fusion | flops 3244294144 | bytes 2427392 | tf_op jit(solution)/shard_map/while/body/eval_jaxpr/dot_general | solution.py:54
  374.3 9.8 %fusion.151 = f32[32,512,128]{2,1,0:T(8,128)} fusion(f32[32,512,128]{2,1,0:T(8,128)} %get-tuple-element.436, s32[]{:T(128)} %get-tuple-element.435, f32[4096,128]{1,0:T(8,128)S(1)} %get-tuple-element.446, s32[4096]{0:T(1024)S(1)} %bitcast.180, s32[4096]{0:T(1024)S(1)} %bitcast.181, s32[4096]{0:T(1024)S(1)} %bitcast.182, s32[4096]{0:T(1024)S(1)} %bitcast.179, ...), kind=kOutput, calls=%fused_computation.18.clone.1 | convolution fusion | flops 3244294144 | bytes 2427392 | tf_op jit(solution)/shard_map/while/body/eval_jaxpr/dot_general | solution.py:54
  386.5 9.8 %fusion.151 = f32[32,512,128]{2,1,0:T(8,128)} fusion(f32[32,512,128]{2,1,0:T(8,128)} %get-tuple-element.436, s32[]{:T(128)} %get-tuple-element.435, f32[4096,128]{1,0:T(8,128)S(1)} %get-tuple-element.446, s32[4096]{0:T(1024)S(1)} %bitcast.180, s32[4096]{0:T(1024)S(1)} %bitcast.181, s32[4096]{0:T(1024)S(1)} %bitcast.182, s32[4096]{0:T(1024)S(1)} %bitcast.179, ...), kind=kOutput, calls=%fused_computation.18.clone.1 | convolution fusion | flops 3244294144 | bytes 2427392 | tf_op jit(solution)/shard_map/while/body/eval_jaxpr/dot_general | solution.py:54
  398.6 9.9 %fusion.151 = f32[32,512,128]{2,1,0:T(8,128)} fusion(f32[32,512,128]{2,1,0:T(8,128)} %get-tuple-element.436, s32[]{:T(128)} %get-tuple-element.435, f32[4096,128]{1,0:T(8,128)S(1)} %get-tuple-element.446, s32[4096]{0:T(1024)S(1)} %bitcast.180, s32[4096]{0:T(1024)S(1)} %bitcast.181, s32[4096]{0:T(1024)S(1)} %bitcast.182, s32[4096]{0:T(1024)S(1)} %bitcast.179, ...), kind=kOutput, calls=%fused_computation.18.clone.1 | convolution fusion | flops 3244294144 | bytes 2427392 | tf_op jit(solution)/shard_map/while/body/eval_jaxpr/dot_general | solution.py:54
  410.8 9.8 %fusion.151 = f32[32,512,128]{2,1,0:T(8,128)} fusion(f32[32,512,128]{2,1,0:T(8,128)} %get-tuple-element.436, s32[]{:T(128)} %get-tuple-element.435, f32[4096,128]{1,0:T(8,128)S(1)} %get-tuple-element.446, s32[4096]{0:T(1024)S(1)} %bitcast.180, s32[4096]{0:T(1024)S(1)} %bitcast.181, s32[4096]{0:T(1024)S(1)} %bitcast.182, s32[4096]{0:T(1024)S(1)} %bitcast.179, ...), kind=kOutput, calls=%fused_computation.18.clone.1 | convolution fusion | flops 3244294144 | bytes 2427392 | tf_op jit(solution)/shard_map/while/body/eval_jaxpr/dot_general | solution.py:54
  422.9 9.8 %fusion.151 = f32[32,512,128]{2,1,0:T(8,128)} fusion(f32[32,512,128]{2,1,0:T(8,128)} %get-tuple-element.436, s32[]{:T(128)} %get-tuple-element.435, f32[4096,128]{1,0:T(8,128)S(1)} %get-tuple-element.446, s32[4096]{0:T(1024)S(1)} %bitcast.180, s32[4096]{0:T(1024)S(1)} %bitcast.181, s32[4096]{0:T(1024)S(1)} %bitcast.182, s32[4096]{0:T(1024)S(1)} %bitcast.179, ...), kind=kOutput, calls=%fused_computation.18.clone.1 | convolution fusion | flops 3244294144 | bytes 2427392 | tf_op jit(solution)/shard_map/while/body/eval_jaxpr/dot_general | solution.py:54
  435.1 9.8 %fusion.151 = f32[32,512,128]{2,1,0:T(8,128)} fusion(f32[32,512,128]{2,1,0:T(8,128)} %get-tuple-element.436, s32[]{:T(128)} %get-tuple-element.435, f32[4096,128]{1,0:T(8,128)S(1)} %get-tuple-element.446, s32[4096]{0:T(1024)S(1)} %bitcast.180, s32[4096]{0:T(1024)S(1)} %bitcast.181, s32[4096]{0:T(1024)S(1)} %bitcast.182, s32[4096]{0:T(1024)S(1)} %bitcast.179, ...), kind=kOutput, calls=%fused_computation.18.clone.1 | convolution fusion | flops 3244294144 | bytes 2427392 | tf_op jit(solution)/shard_map/while/body/eval_jaxpr/dot_general | solution.py:54
  447.2 9.8 %fusion.151 = f32[32,512,128]{2,1,0:T(8,128)} fusion(f32[32,512,128]{2,1,0:T(8,128)} %get-tuple-element.436, s32[]{:T(128)} %get-tuple-element.435, f32[4096,128]{1,0:T(8,128)S(1)} %get-tuple-element.446, s32[4096]{0:T(1024)S(1)} %bitcast.180, s32[4096]{0:T(1024)S(1)} %bitcast.181, s32[4096]{0:T(1024)S(1)} %bitcast.182, s32[4096]{0:T(1024)S(1)} %bitcast.179, ...), kind=kOutput, calls=%fused_computation.18.clone.1 | convolution fusion | flops 3244294144 | bytes 2427392 | tf_op jit(solution)/shard_map/while/body/eval_jaxpr/dot_general | solution.py:54
  459.4 9.9 %fusion.151 = f32[32,512,128]{2,1,0:T(8,128)} fusion(f32[32,512,128]{2,1,0:T(8,128)} %get-tuple-element.436, s32[]{:T(128)} %get-tuple-element.435, f32[4096,128]{1,0:T(8,128)S(1)} %get-tuple-element.446, s32[4096]{0:T(1024)S(1)} %bitcast.180, s32[4096]{0:T(1024)S(1)} %bitcast.181, s32[4096]{0:T(1024)S(1)} %bitcast.182, s32[4096]{0:T(1024)S(1)} %bitcast.179, ...), kind=kOutput, calls=%fused_computation.18.clone.1 | convolution fusion | flops 3244294144 | bytes 2427392 | tf_op jit(solution)/shard_map/while/body/eval_jaxpr/dot_general | solution.py:54
  471.5 9.8 %fusion.151 = f32[32,512,128]{2,1,0:T(8,128)} fusion(f32[32,512,128]{2,1,0:T(8,128)} %get-tuple-element.436, s32[]{:T(128)} %get-tuple-element.435, f32[4096,128]{1,0:T(8,128)S(1)} %get-tuple-element.446, s32[4096]{0:T(1024)S(1)} %bitcast.180, s32[4096]{0:T(1024)S(1)} %bitcast.181, s32[4096]{0:T(1024)S(1)} %bitcast.182, s32[4096]{0:T(1024)S(1)} %bitcast.179, ...), kind=kOutput, calls=%fused_computation.18.clone.1 | convolution fusion | flops 3244294144 | bytes 2427392 | tf_op jit(solution)/shard_map/while/body/eval_jaxpr/dot_general | solution.py:54
  481.5 2.4 multiply_reduce_fusion
  484.4 1.6 rsqrt_multiply_fusion
  486.1 2.9 divide_subtract_fusion
  489.0 70.4 %reduce-scatter.2.cloned.1.call-done = f32[4096,128]{1,0:T(8,128)} async-done(((f32[16384,128]{1,0:T(8,128)}), f32[4096,128]{1,0:T(8,128)}) %reduce-scatter.2.cloned.1.call-update) | async-done | bytes 2097168 | tf_op jit(solution)/shard_map/reduce_scatter | solution.py:107
  559.4 2.4 multiply_reduce_fusion.1
  562.4 3.1 divide_subtract_fusion.1
  (192 shorter events, 63.5 us)
Async XLA Ops:
  8.0 16.2 %copy-start = (bf16[512,3456]{1,0:T(8,128)(2,1)S(1)}, bf16[512,3456]{1,0:T(8,128)(2,1)}, u32[]{:S(2)}) copy-start(bf16[512,3456]{1,0:T(8,128)(2,1)} %param.29) | copy-start | bytes 10616836
  10.7 43.7 %all-to-all-start = ((s32[32,128,4]{1,2,0:T(4,128)}), s32[32,128,4]{1,2,0:T(4,128)}, u32[]{:S(2)}, u32[]{:S(2)}) async-start(s32[32,128,4]{1,2,0:T(4,128)} %copy.46), calls=%async_computation | async-start | bytes 131072 | tf_op jit(solution)/shard_map/all_to_all | solution.py:102
  20.6 3.6 copy-start.15
  24.2 1.2 copy-start.2
  24.2 1.2 copy-start.20
  24.9 2.1 copy-start.12
  28.3 4.1 copy-start.10
  28.3 4.1 copy-start.4
  33.2 1.0 copy-start.18
  37.7 4.5 copy-start.7
  41.3 1.0 copy-start.9
  47.7 1.6 copy-start.19
  54.3 7.5 %copy-start.3 = (bf16[128,3456]{1,0:T(8,128)(2,1)S(1)}, bf16[128,3456]{1,0:T(8,128)(2,1)}, u32[]{:S(2)}) copy-start(bf16[128,3456]{1,0:T(8,128)(2,1)} %param.26) | copy-start | bytes 2654212
  54.3 7.5 %copy-start.11 = (bf16[128,512]{1,0:T(8,128)(2,1)S(1)}, bf16[128,512]{1,0:T(8,128)(2,1)}, u32[]{:S(2)}) copy-start(bf16[128,512]{1,0:T(8,128)(2,1)} %copy-done.10) | copy-start | bytes 393220
  54.3 38.2 %all-to-all-start.1 = ((f32[32,128,128]{2,1,0:T(8,128)}), f32[32,128,128]{2,1,0:T(8,128)S(1)}, u32[]{:S(2)}, u32[]{:S(2)}) async-start(f32[32,128,128]{2,1,0:T(8,128)} %copy.49), calls=%async_computation.1 | async-start | bytes 4194304 | tf_op jit(solution)/shard_map/all_to_all | solution.py:101
  61.8 419.6 %all-reduce.5.cloned.1.call-start = ((), (), s32[]{:S(2)}) async-start(), calls=%async_computation.4 | async-start | bytes 32505856 | tf_op jit(solution)/shard_map/psum | solution.py:134
  65.9 5.2 copy-start.8
  73.8 485.6 %reduce-scatter.2.cloned.1.call-start = ((), (), s32[]{:S(2)}) async-start(), calls=%async_computation.3 | async-start | bytes 10485760 | tf_op jit(solution)/shard_map/reduce_scatter | solution.py:107
  481.4 2.4 copy-start.16
  481.4 3.0 copy-start.13
  481.4 3.0 copy-start.14
  481.4 4.6 copy-start.5
  489.0 72.8 %copy-start.17 = (f32[4096]{0:T(1024)S(1)}, f32[4096]{0:T(1024)}, u32[]{:S(2)}) copy-start(f32[4096]{0:T(1024)} %param.37) | copy-start | bytes 49156
  559.4 3.0 copy-start.6
  562.4 3.1 copy-start.1
Sparse Core Ops, SparseCore 0:
  73.9 220.3 all-reduce.4
Sparse Core Ops, SparseCore 1:
  481.5 77.9 reduce-scatter.1
where the time goes:
time: 576 us; the launch traced here: 573 us
  matrix products  340 us (59%)
  waiting for transfers between devices  89 us (15%)
  local copies, waits for them, and re-layouts  65.9 us (11%)
  loops' own time  26.7 us (5%)
  other arithmetic  18.3 us (3%)
  between operations  16.5 us (3%)
  starting transfers between devices  16.3 us (3%)
    dot_general x40, matrix products, one_block(): return jnp.dot(counts, grads, precision=lax.Precision.HIGHEST)  322 us
    reduce_scatter x1, waiting for transfers between devices, on_device(): lax.psum_scatter(host_grad, 'local', scatter_dimension=0, tiled=True)  70.4 us
    slice x32, local copies, waits for them, and re-layouts, one_block(): row_ids[None, :, pooled] == wanted[:, None]  33.8 us
    another operation x5, loops' own time, pooled_rows(): blocks = lax.map(one_block, jnp.arange(block_count, dtype=jnp.int32))  26.7 us
    dynamic_slice x40, local copies, waits for them, and re-layouts, pooled_rows(): blocks = lax.map(one_block, jnp.arange(block_count, dtype=jnp.int32))  23.5 us
    all_to_all x1, waiting for transfers between devices, on_device(): lax.all_to_all(send_grads, 'hst', split_axis=0, concat_axis=0, tiled=True)  18.6 us
  transfers between devices with their start and end apart: 4, of which 2 were waited for; matrix products, arithmetic and copies ran while one was open for 72% of the time, Pallas kernels for 0%

commit v1 on v0

--- a/solution.py
+++ b/solution.py
@@ -1,8 +1,10 @@
-import math
+import functools
 
 import jax
 import jax.numpy as jnp
 from jax import lax
+from jax.experimental import pallas as pl
+from jax.experimental.pallas import tpu as pltpu
 from jax.sharding import PartitionSpec as P
 
 TS = 22
@@ -42,19 +44,46 @@
     return (stored - LEARN_RATE * grads / jnp.sqrt(accum_new)[:, None], accum_new)
 
 
+def pooled_kernel(row_total, ids, grads, out, *sums):
+    step = min(row_total, 256)
+
+    @pl.loop(0, row_total // step)
+    def _(i):
+        rows = pl.ds(pl.multiple_of(i * step, step), step)
+        for total in sums:
+            total[rows, :] = jnp.zeros((step, total.shape[1]), jnp.float32)
+
+    @pl.loop(0, grads.shape[0] // 8)
+    def _(group):
+        for pair in range(4):
+            sample = group * 8 + pair * 2
+            first = grads[pl.ds(sample, 1), :]
+            second = grads[pl.ds(sample + 1, 1), :]
+            at = [ids[sample * HOT + k] for k in range(2 * HOT)]
+            held = [sums[k % HOT][pl.ds(at[k], 1), :] for k in range(2 * HOT)]
+            new = [held[k] + first for k in range(HOT)]
+            for k in range(HOT):
+                new.append(jnp.where(at[k] == at[HOT + k], new[k], held[HOT + k]) + second)
+            for k in range(2 * HOT):
+                sums[k % HOT][pl.ds(at[k], 1), :] = new[k]
+
+    @pl.loop(0, row_total // step)
+    def _(i):
+        rows = pl.ds(pl.multiple_of(i * step, step), step)
+        out[rows, :] = (sums[0][rows, :] + sums[1][rows, :]) + (sums[2][rows, :] + sums[3][rows, :])
+
+
 def pooled_rows(row_ids, grads, row_total):
-    block = math.gcd(row_total, 512)
-    block_count = row_total // block
-
-    def one_block(block_index):
-        wanted = block_index * block + jnp.arange(block, dtype=jnp.int32)
-        counts = jnp.zeros((block, row_ids.shape[0]), jnp.float32)
-        for pooled in range(row_ids.shape[1]):
-            counts = counts + (row_ids[None, :, pooled] == wanted[:, None]).astype(jnp.float32)
-        return jnp.dot(counts, grads, precision=lax.Precision.HIGHEST)
-
-    blocks = lax.map(one_block, jnp.arange(block_count, dtype=jnp.int32))
-    return blocks.reshape(row_total, grads.shape[1])
+    width = grads.shape[1]
+    return pl.pallas_call(
+        functools.partial(pooled_kernel, row_total),
+        out_shape=jax.ShapeDtypeStruct((row_total, width), jnp.float32),
+        in_specs=[pl.BlockSpec(memory_space=pltpu.SMEM), pl.BlockSpec(memory_space=pltpu.VMEM)],
+        out_specs=pl.BlockSpec(memory_space=pltpu.VMEM),
+        scratch_shapes=[pltpu.VMEM((row_total, width), jnp.float32)] * HOT,
+        compiler_params=pltpu.CompilerParams(vmem_limit_bytes=48 << 20),
+        name="pooled_rows",
+    )(row_ids.reshape(-1), grads)
 
 
 def on_device(
@@ -127,9 +156,9 @@
     down_step = down_grad / jnp.sqrt(down_acc + down_grad * down_grad)
     up_step = up_grad / jnp.sqrt(up_acc + up_grad * up_grad)
     small_grads = feature_grad[:, emb_width * (1 + TS) :].reshape(sample_count, TR, emb_width)
-    small_local = jnp.concatenate(
-        [pooled_rows(small_rows[:, table, :], small_grads[:, table, :], RS) for table in range(TR)],
-        axis=0,
+    small_ids = small_rows + RS * jnp.arange(TR, dtype=jnp.int32)[None, :, None]
+    small_local = pooled_rows(
+        small_ids.reshape(-1, HOT), small_grads.reshape(-1, emb_width), TR * RS
     )
     small_total = lax.psum(small_local, ("hst", "local"))
     small_new, small_acc_new = rowwise_adagrad(small_store, small_acc, small_total)

time: 576 us -> 328 us (0.57)
  matrix products: 340 us -> 18.3 us
  waiting for transfers between devices: 89 us -> 211 us
  local copies, waits for them, and re-layouts: 65.9 us -> 13.7 us
  Pallas kernels: 0 us -> 36.6 us
  loops' own time: 26.7 us -> 0 us
    dot_general x40 -> x0, matrix products: 322 us -> none  [one_block(): return jnp.dot(counts, grads, precision=lax.Precision.HIGHEST)]
    psum x1, waiting for transfers between devices: 0.02 us -> 183 us  [on_device(): small_total = lax.psum(small_local, ('hst', 'local'))]
    reduce_scatter x1, waiting for transfers between devices: 70.4 us -> 0.01 us  [on_device(): lax.psum_scatter(host_grad, 'local', scatter_dimension=0, tiled=True)]
    pallas_call x0 -> x2, Pallas kernels: none -> 36.6 us  [pooled_rows(): pl.pallas_call(functools.partial(pooled_kernel, row_total), out_shape=jax...]
    slice x33 -> x0, local copies, waits for them, and re-layouts: 34.6 us -> none  [the longest x32 33.8 us: one_block(): row_ids[None, :, pooled] == wanted[:, None]]
    another operation x5 -> x0, loops' own time: 26.7 us -> none  [pooled_rows(): blocks = lax.map(one_block, jnp.arange(block_count, dtype=jnp.int32))]
    dynamic_slice x40 -> x0, local copies, waits for them, and re-layouts: 23.5 us -> none  [pooled_rows(): blocks = lax.map(one_block, jnp.arange(block_count, dtype=jnp.int32))]
    all_to_all x1, waiting for transfers between devices: 18.6 us -> 28.3 us  [on_device(): lax.all_to_all(send_grads, 'hst', split_axis=0, concat_axis=0, tiled=True)]
  transfers between devices with their start and end apart: 4 -> 4, of which waited for: 2 -> 3; matrix products, arithmetic and copies ran while one was open for 72% -> 6% of each run, Pallas kernels for 0% -> 9%
where the time goes in v1:
time: 328 us; the launch traced here: 326 us
  waiting for transfers between devices  211 us (64%)
  Pallas kernels  36.6 us (11%)
  matrix products  18.3 us (6%)
  between operations  16.5 us (5%)
  starting transfers between devices  15.7 us (5%)
  other arithmetic  13.9 us (4%)
  local copies, waits for them, and re-layouts  13.7 us (4%)
    psum x1, waiting for transfers between devices, on_device(): small_total = lax.psum(small_local, ('hst', 'local'))  183 us
    pallas_call x2, Pallas kernels, pooled_rows(): pl.pallas_call(functools.partial(pooled_kernel, row_total), out_shape=jax...  36.6 us
    all_to_all x1, waiting for transfers between devices, on_device(): lax.all_to_all(send_grads, 'hst', split_axis=0, concat_axis=0, tiled=True)  28.3 us
    all_to_all x1, starting transfers between devices, on_device(): lax.all_to_all(send_ids, 'hst', split_axis=0, concat_axis=0, tiled=True)  8.42 us
    all_to_all x1, starting transfers between devices, on_device(): lax.all_to_all(send_grads, 'hst', split_axis=0, concat_axis=0, tiled=True)  7.01 us
  transfers between devices with their start and end apart: 4, of which 3 were waited for; matrix products, arithmetic and copies ran while one was open for 6% of the time, Pallas kernels for 9%

profile of v1, /device:TPU:0, one launch (start us, length us, event | category | flops | bytes accessed | tf_op | source)
XLA Modules:
  0.0 326.1 jit_solution(4492231570831516920)
XLA Ops:
  8.0 0.0 copy-start
  8.0 0.0 all-reduce.5.cloned.1.call-start
  8.1 0.9 reshape.51
  9.7 0.0 copy-start.11
  9.8 3.5 %convolution_convert_fusion.1 = bf16[128,512]{1,0:T(8,128)(2,1)S(1)} fusion(bf16[128,3456]{1,0:T(8,128)(2,1)} %param.16, bf16[512,3456]{1,0:T(8,128)(2,1)} %param.18), kind=kOutput, calls=%fused_computation.13 | convolution fusion | flops 453050368 | bytes 4554752 | tf_op jit(solution)/shard_map/dot_general | solution.py:23
  13.3 0.0 copy-done
  13.3 0.0 copy-done.11
  13.3 0.0 copy-start.2
  13.3 0.0 copy-start.16
  13.3 0.7 convolution_add_fusion.1
  14.0 0.0 copy-start.7
  14.1 0.4 copy-done.2
  14.5 0.0 copy-done.16
  14.5 1.6 fusion.8
  16.1 0.0 copy-done.7
  16.1 0.0 copy-start.3
  16.1 1.3 convolution_convert_fusion
  17.4 0.7 copy-done.3
  18.1 0.7 convolution_add_fusion
  18.8 0.0 copy-start.6
  18.8 4.0 %fusion.21 = f32[512,3456]{1,0:T(8,128)} fusion(bf16[128,512]{1,0:T(8,128)(2,1)S(1)} %convolution_convert_fusion, bf16[128,3456]{1,0:T(8,128)(2,1)S(1)} %copy-done.2), kind=kOutput, calls=%fused_computation.44 | convolution fusion | flops 452984832 | bytes 8093696 | tf_op jit(solution)/shard_map/dot_general | solution.py:140
  22.8 4.0 %fusion.9 = f32[512,3456]{1,0:T(8,128)} fusion(bf16[128,512]{1,0:T(8,128)(2,1)S(1)} %convolution_convert_fusion.1, bf16[128,3456]{1,0:T(8,128)(2,1)S(1)} %copy-done.2, f32[3456]{0:T(1024)S(1)} %copy-done.7, f32[128]{0:T(128)S(1)} %fusion.8), kind=kOutput, calls=%fused_computation.21 | convolution fusion | flops 454754304 | bytes 8108032 | tf_op jit(solution)/shard_map/dot_general | solution.py:149
  26.8 0.0 copy-done.6
  26.9 0.0 copy-done.14
  26.9 0.1 broadcast_add_fusion
  26.9 0.2 copy.43
  27.1 0.3 reshape_reshape.10.ids
  27.4 5.7 %pooled_rows.3 = f32[4096,128]{1,0:T(8,128)} custom-call(s32[2048]{0:T(1024)S(1)} %reshape_reshape.10.ids, f32[512,128]{1,0:T(8,128)S(1)} %reshape_reshape.11.grads), custom_call_target="tpu_custom_call" | custom-call | tf_op jit(solution)/shard_map/pooled_rows/pallas_call | solution.py:78
  33.1 0.0 all-reduce.5.cloned.1.call-update
  33.2 0.6 copy-done.15
  33.8 0.1 iota_compare_fusion
  33.9 0.1 copy-done.10
  33.9 0.1 fusion.14
  34.0 0.2 select_reduce_fusion
  34.2 0.7 copy.38
  34.9 8.4 %all-to-all-start = ((s32[32,128,4]{1,2,0:T(4,128)}), s32[32,128,4]{1,2,0:T(4,128)S(1)}, u32[]{:S(2)}, u32[]{:S(2)}) async-start(s32[32,128,4]{1,2,0:T(4,128)} %copy.38), calls=%async_computation | async-start | bytes 131072 | tf_op jit(solution)/shard_map/all_to_all | solution.py:131
  43.3 0.0 slice-done
  43.3 0.4 copy.40
  43.7 1.6 copy.41
  45.4 2.5 fusion.17
  47.9 2.5 copy.42
  50.4 0.4 all-to-all-done
  50.8 7.0 %all-to-all-start.1 = ((f32[32,128,128]{2,1,0:T(8,128)}), f32[32,128,128]{2,1,0:T(8,128)S(1)}, u32[]{:S(2)}, u32[]{:S(2)}) async-start(f32[32,128,128]{2,1,0:T(8,128)} %copy.42), calls=%async_computation.1 | async-start | bytes 4194304 | tf_op jit(solution)/shard_map/all_to_all | solution.py:130
  57.8 0.2 reduce-scatter.2.cloned.1.call-start
  58.0 2.0 copy.39
  60.0 3.3 reshape_reshape.9.ids
  63.3 28.3 %all-to-all-done.1 = f32[32,128,128]{2,1,0:T(8,128)S(1)} async-done(((f32[32,128,128]{2,1,0:T(8,128)}), f32[32,128,128]{2,1,0:T(8,128)S(1)}, u32[]{:S(2)}, u32[]{:S(2)}) %all-to-all-start.1) | async-done | bytes 2097184 | tf_op jit(solution)/shard_map/all_to_all | solution.py:130
  91.5 30.8 %pooled_rows.2 = f32[16384,128]{1,0:T(8,128)} custom-call(s32[16384]{0:T(1024)S(1)} %reshape_reshape.9.ids, f32[4096,128]{1,0:T(8,128)S(1)} %bitcast.35), custom_call_target="tpu_custom_call" | custom-call | tf_op jit(solution)/shard_map/pooled_rows/pallas_call | solution.py:78
  122.3 0.0 reduce-scatter.2.cloned.1.call-update
  122.4 0.0 copy-start.12
  122.4 0.0 copy-start.8
  122.4 0.0 copy-start.9
  122.4 182.7 %all-reduce.5.cloned.1.call-done = (f32[4096,128]{1,0:T(8,128)}, f32[512,3456]{1,0:T(8,128)}, f32[512,3456]{1,0:T(8,128)}) async-done(((f32[4096,128]{1,0:T(8,128)}, f32[512,3456]{1,0:T(8,128)}, f32[512,3456]{1,0:T(8,128)}), (f32[4096,128]{1,0:T(8,128)}, f32[512,3456]{1,0:T(8,128)}, f32[512,3456]{1,0:T(8,128)})) %all-reduce.5.cloned.1.call-update) | async-done | bytes 16252944 | tf_op jit(solution)/shard_map/psum | solution.py:163
  305.1 2.4 multiply_reduce_fusion
  307.5 0.0 copy-done.12
  307.5 0.6 fusion.19
  308.1 0.0 copy-done.8
  308.1 0.0 copy-done.9
  308.1 1.6 rsqrt_multiply_fusion
  309.7 2.9 divide_subtract_fusion
  312.6 2.4 multiply_reduce_fusion.1
  315.0 0.0 copy-done.13
  315.0 0.6 fusion.20
  315.6 3.1 divide_subtract_fusion.1
  (15 shorter events, 0.1 us)
Async XLA Ops:
  8.0 5.3 %copy-start = (bf16[512,3456]{1,0:T(8,128)(2,1)S(1)}, bf16[512,3456]{1,0:T(8,128)(2,1)}, u32[]{:S(2)}) copy-start(bf16[512,3456]{1,0:T(8,128)(2,1)} %param.19) | copy-start | bytes 10616836
  8.0 297.1 %all-reduce.5.cloned.1.call-start = ((), (), s32[]{:S(2)}) async-start(), calls=%async_computation.4 | async-start | bytes 32505856 | tf_op jit(solution)/shard_map/psum | solution.py:163
  9.7 3.6 %copy-start.11 = (f32[3456]{0:T(1024)S(1)}, f32[3456]{0:T(1024)}, u32[]{:S(2)}) copy-start(f32[3456]{0:T(1024)} %param.20) | copy-start | bytes 41476
  13.3 1.2 copy-start.2
  13.3 1.2 copy-start.16
  14.0 2.1 copy-start.7
  16.1 2.0 copy-start.3
  18.8 8.0 %copy-start.6 = (f32[128,3456]{1,0:T(8,128)}, f32[128,3456]{1,0:T(8,128)S(1)}, u32[]{:S(2)}) copy-start(f32[128,3456]{1,0:T(8,128)S(1)} %convolution_add_fusion) | copy-start | bytes 5308420
  22.8 4.1 %copy-start.14 = (s32[128,4,4]{0,2,1:T(4,128)S(1)}, s32[128,4,4]{0,2,1:T(4,128)}, u32[]{:S(2)}) copy-start(s32[128,4,4]{0,2,1:T(4,128)} %param.25) | copy-start | bytes 24580
  33.1 0.7 copy-start.15
  33.1 0.8 copy-start.10
  33.8 9.5 %slice-start = ((f32[128,3456]{1,0:T(8,128)}), f32[128,2816]{1,0:T(8,128)S(1)}, s32[]{:S(2)}) async-start(f32[128,3456]{1,0:T(8,128)} %copy-done.6), calls=%async_computation.5 | async-start | bytes 2883584 | tf_op jit(solution)/shard_map/slice | solution.py:117
  34.9 15.9 %all-to-all-start = ((s32[32,128,4]{1,2,0:T(4,128)}), s32[32,128,4]{1,2,0:T(4,128)S(1)}, u32[]{:S(2)}, u32[]{:S(2)}) async-start(s32[32,128,4]{1,2,0:T(4,128)} %copy.38), calls=%async_computation | async-start | bytes 131072 | tf_op jit(solution)/shard_map/all_to_all | solution.py:131
  50.8 40.7 %all-to-all-start.1 = ((f32[32,128,128]{2,1,0:T(8,128)}), f32[32,128,128]{2,1,0:T(8,128)S(1)}, u32[]{:S(2)}, u32[]{:S(2)}) async-start(f32[32,128,128]{2,1,0:T(8,128)} %copy.42), calls=%async_computation.1 | async-start | bytes 4194304 | tf_op jit(solution)/shard_map/all_to_all | solution.py:130
  57.8 254.8 %reduce-scatter.2.cloned.1.call-start = ((), (), s32[]{:S(2)}) async-start(), calls=%async_computation.3 | async-start | bytes 10485760 | tf_op jit(solution)/shard_map/reduce_scatter | solution.py:136
  122.4 185.1 %copy-start.12 = (f32[4096]{0:T(1024)S(1)}, f32[4096]{0:T(1024)}, u32[]{:S(2)}) copy-start(f32[4096]{0:T(1024)} %param.29) | copy-start | bytes 49156
  122.4 185.7 %copy-start.8 = (f32[4,3456]{1,0:T(4,128)S(1)}, f32[4,3456]{1,0:T(4,128)}, u32[]{:S(2)}) copy-start(f32[4,3456]{1,0:T(4,128)} %param.31) | copy-start | bytes 165892
  122.4 185.7 %copy-start.9 = (f32[4,3456]{1,0:T(4,128)S(1)}, f32[4,3456]{1,0:T(4,128)}, u32[]{:S(2)}) copy-start(f32[4,3456]{1,0:T(4,128)} %param.30) | copy-start | bytes 165892
  305.1 4.6 %copy-start.4 = (f32[4096,128]{1,0:T(8,128)S(1)}, f32[4096,128]{1,0:T(8,128)}, u32[]{:S(2)}) copy-start(f32[4096,128]{1,0:T(8,128)} %get-tuple-element.6) | copy-start | bytes 6291460
  312.6 2.4 copy-start.13
  312.6 3.0 copy-start.5
  315.6 3.1 copy-start.1
Sparse Core Ops, SparseCore 0:
  33.3 271.7 all-reduce.4
Sparse Core Ops, SparseCore 1:
  122.5 86.0 reduce-scatter.1

commit v2 on v0

v2 whole, which is shorter than its diff:
```python
import functools

import jax
import jax.numpy as jnp
from jax import lax
from jax.experimental import pallas as pl
from jax.experimental.pallas import tpu as pltpu
from jax.sharding import PartitionSpec as P

TS = 22
TR = 4
RS = 1024
HOT = 4
SHARD = 4096
EMB = 128
RANK = 512
WIDTH = 3456
HOSTS = 32
LOCALS = 4
SAMPLES = 128
PACK = SAMPLES + 8
CUT = 1792
LEARN_RATE = 0.05
MESH = pl.DeviceIdType.MESH
F32 = jnp.float32
BF16 = jnp.bfloat16


def product(left, right, left_dim=1, right_dim=0):
    return lax.dot_general(
        left, right, (((left_dim,), (right_dim,)), ((), ())), preferred_element_type=F32
    )


def diagonal():
    return lax.broadcasted_iota(jnp.int32, (128, 128), 0) == lax.broadcasted_iota(
        jnp.int32, (128, 128), 1
    )


def dense_kernel(
    features, labels, bias, head, head_bias, place, bags, down_hbm, up_hbm,
    send, small, rights, lows, down, up, cross, sems,
):
    down_copy = pltpu.make_async_copy(down_hbm, down, sems.at[0])
    up_copy = pltpu.make_async_copy(up_hbm, up, sems.at[1])
    down_copy.start()
    up_copy.start()

    @pl.loop(0, HOSTS)
    def _(slot):
        send[slot] = jnp.zeros((PACK, EMB), F32)

    rights[0:SAMPLES, :] = features[...]
    parts = [(start, min(256, WIDTH - start)) for start in range(0, WIDTH, 256)]
    down_copy.wait()
    low_proj = product(features[...], down[...], 1, 1).astype(BF16)
    lows[SAMPLES:, :] = low_proj
    up_copy.wait()
    terms = jnp.zeros((SAMPLES, 128), F32)
    for start, width in parts:
        at = pl.ds(start, width)
        out = product(low_proj, up[:, at]) + bias[:, at]
        cross[:, at] = out
        wide = features[:, at].astype(F32)
        weighted = (wide * out + wide) * head[:, at]
        for tile in range(width // 128):
            terms = terms + weighted[:, tile * 128 : (tile + 1) * 128]
    logit = jnp.sum(terms, axis=1, keepdims=True) + head_bias[0]
    label = jnp.sum(
        jnp.where(diagonal(), labels[...].astype(F32), 0.0), axis=1, keepdims=True
    )
    logit_grad = jax.nn.sigmoid(logit) - label
    for start, width in parts:
        at = pl.ds(start, width)
        layer_grad = logit_grad * head[:, at]
        rights[SAMPLES:, at] = (layer_grad * features[:, at].astype(F32)).astype(BF16)
    low_grad = product(rights[SAMPLES:, :], up[...], 1, 1).astype(BF16)
    lows[0:SAMPLES, :] = low_grad
    for start, width in parts:
        at = pl.ds(start, width)
        layer_grad = logit_grad * head[:, at]
        grad = layer_grad * (cross[:, at] + 1.0) + product(low_grad, down[:, at])
        for tile in range(width // 128):
            piece = grad[:, tile * 128 : (tile + 1) * 128]
            table = start // 128 + tile - 1
            if 0 <= table < TS:
                slot = place[table]
                send[slot, 0:SAMPLES, :] = piece
                send[slot, SAMPLES:, :] = bags[table]
            elif table >= TS:
                small[:, (table - TS) * EMB : (table - TS + 1) * EMB] = piece


def exchange_kernel(
    send, rights, lows, small, small_ids,
    got, ids, dense, small_sum,
    left_own, left_other, own, other, arrived, split, sems, core_sems, out_sems, own_sem,
):
    host = lax.axis_index("hst")
    core = lax.rem(host, 2)
    partner = host + 1 - 2 * core
    barrier = pltpu.get_barrier_semaphore()

    @pl.loop(1, HOSTS)
    def _(off):
        pl.semaphore_signal(
            barrier, inc=1, device_id={"hst": lax.rem(host + off, HOSTS)}, device_id_type=MESH
        )

    pl.semaphore_wait(barrier, HOSTS - 1)

    def bag_copy(off, to, slot):
        return pltpu.make_async_remote_copy(
            src_ref=send.at[to],
            dst_ref=got.at[slot],
            send_sem=sems.at[0, off],
            recv_sem=sems.at[1, off],
            device_id={"hst": to},
            device_id_type=MESH,
        )

    @pl.loop(1, HOSTS)
    def _(off):
        bag_copy(off, lax.rem(host + off, HOSTS), host).start()

    mine = pltpu.make_async_copy(send.at[host], got.at[host], own_sem)
    mine.start()

    def spread(target, left):
        row = lax.broadcasted_iota(jnp.int32, (RANK, RANK), 0)
        rank = lax.broadcasted_iota(jnp.int32, (RANK, RANK), 1)
        place = row & 7
        base = ((row >> 5) * 2 + target) * 16 + ((row >> 3) & 3) * 4
        for part in range(2):
            want = jnp.where((place >> 2) == part, base + place - 4 * part, -1)
            chosen = jnp.where(want == rank, 1.0, 0.0).astype(BF16)
            left[:, part * SAMPLES : (part + 1) * SAMPLES] = product(
                chosen, lows[part * SAMPLES : (part + 1) * SAMPLES, :], 1, 1
            ).astype(BF16)

    def grads(left, out, group):
        @pl.loop(0, WIDTH // 384)
        def _(part):
            at = pl.ds(pl.multiple_of(part * 384, 384), 384)
            out[group * 128 : (group + 1) * 128, at] = product(
                left[group * 128 : (group + 1) * 128, :], rights[:, at]
            )

    def core_copy(group):
        rows = pl.ds(group * 128, 128)
        return pltpu.make_async_remote_copy(
            src_ref=other.at[rows],
            dst_ref=arrived.at[rows],
            send_sem=core_sems.at[0, group],
            recv_sem=core_sems.at[1, group],
            device_id={"hst": partner},
            device_id_type=MESH,
        )

    def out_copy(group):
        rows = pl.ds(group * 128, 128)
        return pltpu.make_async_copy(own.at[rows], dense.at[rows], out_sems.at[group])

    spread(1 - core, left_other)
    for group in range(4):
        grads(left_other, other, group)
        core_copy(group).start()
    spread(core, left_own)
    for group in range(4):
        grads(left_own, own, group)

    for table in range(TR):
        value = small[:, table * EMB : (table + 1) * EMB]
        high = value.astype(BF16)
        split[table, :, 0:EMB] = high
        split[table, :, EMB:] = (value - high.astype(F32)).astype(BF16)

    @pl.loop(0, TR * RS // 128)
    def _(block):
        table = block // 8
        rows = (block % 8) * 128 + lax.broadcasted_iota(jnp.int32, (128, SAMPLES), 0)
        wanted = small_ids[table]
        counts = jnp.zeros((128, SAMPLES), F32)
        for k in range(HOT):
            counts = counts + jnp.where(rows == wanted[k : k + 1, :], 1.0, 0.0)
        both = product(counts.astype(BF16), split[table])
        small_sum[pl.ds(pl.multiple_of(block * 128, 128), 128), :] = both[:, 0:EMB] + both[:, EMB:]

    for group in range(4):
        core_copy(group).wait_recv()

        @pl.loop(0, 4)
        def _(part):
            rows = pl.ds(pl.multiple_of(group * 128 + part * 32, 32), 32)
            own[rows, :] = own[rows, :] + arrived[rows, :]

        out_copy(group).start()

    mine.wait()

    @pl.loop(1, HOSTS)
    def _(off):
        bag_copy(off, lax.rem(host + off, HOSTS), lax.rem(host - off + HOSTS, HOSTS)).wait_recv()

    @pl.loop(0, HOSTS // 2)
    def _(pair):
        low = got[pair * 2, pl.ds(SAMPLES, 8), :]
        high = got[pair * 2 + 1, pl.ds(SAMPLES, 8), :]
        ids[pl.ds(pl.multiple_of(pair * 8, 8), 8), :] = jnp.concatenate(
            [low[0:HOT], high[0:HOT]], axis=0
        ).astype(jnp.int32)

    @pl.loop(1, HOSTS)
    def _(off):
        bag_copy(off, lax.rem(host + off, HOSTS), host).wait_send()

    for group in range(4):
        core_copy(group).wait_send()
        out_copy(group).wait()


def pooled_kernel(ids, grads, out, *sums):
    row_total = out.shape[0]
    step = 256

    @pl.loop(0, row_total // step)
    def _(i):
        rows = pl.ds(pl.multiple_of(i * step, step), step)
        for total in sums:
            total[rows, :] = jnp.zeros((step, EMB), F32)

    @pl.loop(0, HOSTS)
    def _(source):
        @pl.loop(0, SAMPLES // 16)
        def _(group):
            for pair in range(8):
                sample = group * 16 + pair * 2
                first = grads[source, pl.ds(sample, 1), :]
                second = grads[source, pl.ds(sample + 1, 1), :]
                at = [
                    ids[(source * HOT + k % HOT) * SAMPLES + sample + k // HOT]
                    for k in range(2 * HOT)
                ]
                held = [sums[k % HOT][pl.ds(at[k], 1), :] for k in range(2 * HOT)]
                new = [held[k] + first for k in range(HOT)]
                for k in range(HOT):
                    new.append(jnp.where(at[k] == at[HOT + k], new[k], held[HOT + k]) + second)
                for k in range(2 * HOT):
                    sums[k % HOT][pl.ds(at[k], 1), :] = new[k]

    @pl.loop(0, row_total // step)
    def _(i):
        rows = pl.ds(pl.multiple_of(i * step, step), step)
        out[rows, :] = (sums[0][rows, :] + sums[1][rows, :]) + (sums[2][rows, :] + sums[3][rows, :])


class Ring:
    def __init__(self, place, right, left, sent, held, near, passed, sems, chunks=1):
        self.place, self.right, self.left = place, right, left
        self.sent, self.held, self.near, self.passed, self.sems = sent, held, near, passed, sems
        self.chunks = chunks

    def piece(self, ref, chunk):
        if self.chunks == 1:
            return ref
        rows = ref.shape[0] // self.chunks
        return ref.at[pl.ds(chunk * rows, rows)]

    def copy(self, src, dst, index, to):
        return pltpu.make_async_remote_copy(
            src_ref=src, dst_ref=dst, send_sem=self.sems.at[0, index],
            recv_sem=self.sems.at[1, index], device_id=to, device_id_type=MESH,
        )

    def far(self, side, chunk):
        src = self.sent(lax.rem(self.place + 2, 4), side)
        to = self.left if side else self.right
        return self.copy(
            self.piece(src, chunk), self.piece(self.passed[side], chunk),
            2 + side * self.chunks + chunk, to,
        )

    def direct(self, side):
        to = self.left if side else self.right
        target = lax.rem(self.place + (3 if side else 1), 4)
        return self.copy(self.sent(target, 1 - side), self.near[side], side, to)

    def relay(self, side, chunk, sums):
        to = self.left if side else self.right
        return self.copy(
            self.piece(self.passed[side], chunk), self.piece(sums[side], chunk),
            2 + (2 + side) * self.chunks + chunk, to,
        )

    def start(self):
        for chunk in range(self.chunks):
            self.far(0, chunk).start()
            self.far(1, chunk).start()
        self.direct(0).start()
        self.direct(1).start()

    def middle(self, sums):
        for chunk in range(self.chunks):
            for side in range(2):
                self.far(side, chunk).wait_recv()
                target = lax.rem(self.place + (3 if side else 1), 4)
                add_into(self.piece(self.passed[side], chunk), self.piece(self.held(target, side), chunk))
                self.relay(side, chunk, sums).start()

    def drain(self, sums):
        for side in range(2):
            self.direct(side).wait_send()
            for chunk in range(self.chunks):
                self.far(side, chunk).wait_send()
                self.relay(side, chunk, sums).wait_send()


def blocks_of(shape):
    if len(shape) == 3:
        return shape[0], lambda ref, i: ref.at[i]
    rows = min(shape[0], 32 if shape[1] > 256 else 128)
    return shape[0] // rows, lambda ref, i: ref.at[pl.ds(pl.multiple_of(i * rows, rows), rows)]


def add_into(total, term):
    count, at = blocks_of(total.shape)

    @pl.loop(0, count)
    def _(i):
        at(total, i)[...] = at(total, i)[...] + at(term, i)[...]


def add_three(out, first, second, third):
    count, at = blocks_of(out.shape)

    @pl.loop(0, count)
    def _(i):
        at(out, i)[...] = at(first, i)[...] + at(second, i)[...] + at(third, i)[...]


CHUNKS = 4


def reduce_kernel(
    tables, dense, store_hbm, acc, down_acc, up_acc,
    table_new, acc_new, down_step, up_step,
    store, mine, ahead, behind, grads,
    t_near0, t_near1, t_pass0, t_pass1, t_sum0, t_sum1,
    a_near0, a_near1, a_pass0, a_pass1, a_sum0, a_sum1,
    b_near0, b_near1, b_pass0, b_pass1, b_sum0, b_sum1,
    c_near0, c_near1, c_pass0, c_pass1, c_sum0, c_sum1,
    d_near0, d_near1, d_pass0, d_pass1, d_sum0, d_sum1,
    e_near0, e_near1, e_pass0, e_pass1, e_sum0, e_sum1,
    a_out, b_out, c_out, d_out,
    t_sems, r_sems, local_sems,
):
    host = lax.axis_index("hst")
    x = lax.axis_index("local")
    z, y, core = host // 8, (host // 2) % 4, host % 2

    def on_z(step):
        return {"hst": (lax.rem(z + step, 4) * 4 + y) * 2 + core}

    def on_y(step):
        return {"hst": (z * 4 + lax.rem(y + step, 4)) * 2 + core}

    def on_x(step):
        return {"local": lax.rem(x + step, 4)}

    barrier = pltpu.get_barrier_semaphore()
    for neighbours in (on_x, on_y, on_z):
        for step in (1, 3):
            pl.semaphore_signal(
                barrier, inc=1, device_id=neighbours(step), device_id_type=MESH
            )
    half = SHARD // 2
    right, left = lax.rem(x + 1, 4), lax.rem(x + 3, 4)
    locals_ = [
        pltpu.make_async_copy(tables.at[right, pl.ds(0, half)], ahead, local_sems.at[0]),
        pltpu.make_async_copy(tables.at[left, pl.ds(half, half)], behind, local_sems.at[1]),
        pltpu.make_async_copy(dense, grads, local_sems.at[2]),
        pltpu.make_async_copy(tables.at[x], mine, local_sems.at[3]),
        pltpu.make_async_copy(store_hbm, store, local_sems.at[4]),
    ]
    for copy in locals_:
        copy.start()
    pl.semaphore_wait(barrier, 6)

    first = {0: pl.ds(0, 896), 1: pl.ds(896, 896)}
    second = {0: pl.ds(CUT, 896), 1: pl.ds(CUT + 896, 768)}
    inner = {0: pl.ds(0, 896), 1: pl.ds(896, 768)}
    table_ring = Ring(
        x, on_x(1), on_x(3),
        lambda t, s: tables.at[t, pl.ds(s * half, half)],
        lambda t, s: behind if s else ahead,
        (t_near0, t_near1), (t_pass0, t_pass1), t_sems, CHUNKS,
    )
    table_sums = (t_sum0, t_sum1)
    a_ring = Ring(
        z, on_z(1), on_z(3),
        lambda t, s: dense.at[t, :, :, first[s]],
        lambda t, s: grads.at[t, :, :, first[s]],
        (a_near0, a_near1), (a_pass0, a_pass1), r_sems.at[0],
    )
    b_ring = Ring(
        y, on_y(1), on_y(3),
        lambda t, s: dense.at[:, t, :, second[s]],
        lambda t, s: grads.at[:, t, :, second[s]],
        (b_near0, b_near1), (b_pass0, b_pass1), r_sems.at[1],
    )
    c_at = lambda t, s: a_out.at[t, :, first[s]]
    c_ring = Ring(
        y, on_y(1), on_y(3), c_at, c_at, (c_near0, c_near1), (c_pass0, c_pass1), r_sems.at[2]
    )
    d_at = lambda t, s: b_out.at[t, :, inner[s]]
    d_ring = Ring(
        z, on_z(1), on_z(3), d_at, d_at, (d_near0, d_near1), (d_pass0, d_pass1), r_sems.at[3]
    )
    e_at = lambda t, s: (d_out if s else c_out).at[pl.ds(pl.multiple_of(t * 8, 8), 8)]
    e_ring = Ring(
        x, on_x(1), on_x(3), e_at, e_at, (e_near0, e_near1), (e_pass0, e_pass1), r_sems.at[4]
    )

    a_ring.start()
    b_ring.start()
    table_ring.start()
    for copy in locals_[:3]:
        copy.wait()
    a_ring.middle((a_sum0, a_sum1))
    b_ring.middle((b_sum0, b_sum1))
    table_ring.middle(table_sums)

    def finish(ring, sums, outs, place):
        for side in range(2):
            ring.direct(side).wait_recv()
            ring.relay(side, 0, sums).wait_recv()
        add_three(outs[0], ring.held(place, 0), sums[0], ring.near[1])
        add_three(outs[1], ring.held(place, 1), ring.near[0], sums[1])

    finish(a_ring, (a_sum0, a_sum1), [a_out.at[:, :, first[s]] for s in range(2)], z)
    c_ring.start()
    finish(b_ring, (b_sum0, b_sum1), [b_out.at[:, :, inner[s]] for s in range(2)], y)
    d_ring.start()
    c_ring.middle((c_sum0, c_sum1))
    d_ring.middle((d_sum0, d_sum1))
    finish(c_ring, (c_sum0, c_sum1), [c_out.at[:, first[s]] for s in range(2)], y)
    finish(d_ring, (d_sum0, d_sum1), [d_out.at[:, inner[s]] for s in range(2)], z)
    e_ring.start()
    e_ring.middle((e_sum0, e_sum1))
    for copy in locals_[3:]:
        copy.wait()

    eye = diagonal()

    def update(block, first_term, second_term, third_term):
        rows = pl.ds(pl.multiple_of(block * 128, 128), 128)
        grad = first_term + second_term + third_term
        acc_here = jnp.sum(jnp.where(eye, acc[pl.ds(block, 1), :], 0.0), axis=1, keepdims=True)
        total = acc_here + jnp.sum(grad * grad, axis=1, keepdims=True) * (1.0 / EMB)
        table_new[rows, :] = store[rows, :] - grad * (LEARN_RATE * lax.rsqrt(total))
        acc_new[pl.ds(block, 1), :] = jnp.sum(jnp.where(eye, total, 0.0), axis=0, keepdims=True)

    for side in range(2):
        table_ring.direct(side).wait_recv()
    rows_chunk = half // CHUNKS
    for chunk in range(CHUNKS):
        for side in range(2):
            table_ring.relay(side, chunk, table_sums).wait_recv()
            near = (t_near1, t_near0)[side]

            @pl.loop(0, rows_chunk // 128)
            def _(part):
                inside = pl.ds(pl.multiple_of(chunk * rows_chunk + part * 128, 128), 128)
                block = side * (half // 128) + chunk * (rows_chunk // 128) + part
                rows = pl.ds(pl.multiple_of(block * 128, 128), 128)
                update(block, mine[rows, :], table_sums[side][inside, :], near[inside, :])

    e_sums = (e_sum0, e_sum1)
    for side in range(2):
        e_ring.direct(side).wait_recv()
        e_ring.relay(side, 0, e_sums).wait_recv()
    for side, start, width in ((0, 0, CUT), (1, CUT, WIDTH - CUT)):
        at = pl.ds(start, width)
        near = (e_near1, e_near0)[side]
        total = e_ring.held(x, side)[...] + e_sums[side][...] + near[...]
        for step, sums, rows in ((down_step, down_acc, 0), (up_step, up_acc, 4)):
            grad = total[rows : rows + 4]
            step[:, at] = grad * lax.rsqrt(sums[:, at] + grad * grad)

    table_ring.drain(table_sums)
    a_ring.drain((a_sum0, a_sum1))
    b_ring.drain((b_sum0, b_sum1))
    c_ring.drain((c_sum0, c_sum1))
    d_ring.drain((d_sum0, d_sum1))
    e_ring.drain(e_sums)


def small_kernel(store, acc, grads, new, acc_new):
    eye = diagonal()

    @pl.loop(0, TR * RS // 128)
    def _(block):
        rows = pl.ds(pl.multiple_of(block * 128, 128), 128)
        grad = grads[rows, :]
        acc_here = jnp.sum(jnp.where(eye, acc[pl.ds(block, 1), :], 0.0), axis=1, keepdims=True)
        total = acc_here + jnp.sum(grad * grad, axis=1, keepdims=True) * (1.0 / EMB)
        new[rows, :] = store[rows, :] - grad * (LEARN_RATE * lax.rsqrt(total))
        acc_new[pl.ds(block, 1), :] = jnp.sum(jnp.where(eye, total, 0.0), axis=0, keepdims=True)


def shaped(shape, dtype=F32):
    return jax.ShapeDtypeStruct(shape, dtype)


ANY = pl.BlockSpec(memory_space=pl.ANY)
VMEM = pl.BlockSpec(memory_space=pltpu.VMEM)
SMEM = pl.BlockSpec(memory_space=pltpu.SMEM)
DMA = pltpu.SemaphoreType.DMA


def params(mebibytes, **others):
    return pltpu.CompilerParams(vmem_limit_bytes=mebibytes << 20, **others)


def on_device(
    features, labels, cross_down, cross_up, cross_bias, head_weight, head_bias, table_place,
    bag_rows, small_rows, table_store, table_acc, small_store, small_acc, down_acc, up_acc,
):
    bags = jnp.pad(
        jnp.transpose(bag_rows, (1, 2, 0)).astype(F32), ((0, 0), (0, 8 - HOT), (0, 0))
    )
    small_ids = jnp.transpose(small_rows, (1, 2, 0))
    send, small, rights, lows = pl.pallas_call(
        dense_kernel,
        out_shape=(
            shaped((HOSTS, PACK, EMB)), shaped((SAMPLES, TR * EMB)),
            shaped((2 * SAMPLES, WIDTH), BF16), shaped((2 * SAMPLES, RANK), BF16),
        ),
        in_specs=[VMEM] * 4 + [SMEM] * 2 + [VMEM] + [ANY] * 2,
        out_specs=(VMEM,) * 4,
        scratch_shapes=[
            pltpu.VMEM((RANK, WIDTH), BF16), pltpu.VMEM((RANK, WIDTH), BF16),
            pltpu.VMEM((SAMPLES, WIDTH), F32), DMA((2,)),
        ],
        compiler_params=params(40),
        name="dense_backward",
    )(
        features, labels.reshape(1, -1), cross_bias.reshape(1, -1), head_weight.reshape(1, -1),
        head_bias, table_place, bags, cross_down, cross_up,
    )
    whole = (RANK, WIDTH)
    got, ids, dense, small_sum = pl.pallas_call(
        exchange_kernel,
        out_shape=(
            shaped((HOSTS, PACK, EMB)), shaped((HOSTS * HOT, SAMPLES), jnp.int32),
            shaped(whole), shaped((TR * RS, EMB)),
        ),
        in_specs=[ANY] + [VMEM] * 4,
        out_specs=(VMEM, VMEM, ANY, VMEM),
        scratch_shapes=[
            pltpu.VMEM((RANK, 2 * SAMPLES), BF16), pltpu.VMEM((RANK, 2 * SAMPLES), BF16),
            pltpu.VMEM(whole, F32), pltpu.VMEM(whole, F32), pltpu.VMEM(whole, F32),
            pltpu.VMEM((TR, SAMPLES, 2 * EMB), BF16),
            DMA((2, HOSTS)), DMA((2, 4)), DMA((4,)), DMA,
        ],
        compiler_params=params(48, collective_id=0, has_side_effects=True),
        name="exchange",
    )(send, rights, lows, small, small_ids)
    small_total = lax.psum(small_sum, ("hst", "local"))
    tables = pl.pallas_call(
        pooled_kernel,
        out_shape=shaped((LOCALS * SHARD, EMB)),
        in_specs=[SMEM, VMEM],
        out_specs=VMEM,
        scratch_shapes=[pltpu.VMEM((LOCALS * SHARD, EMB), F32)] * HOT,
        compiler_params=params(50),
        name="pooled_rows",
    )(ids.reshape(-1), got)

    def ring_buffers(first_shape, second_shape):
        near = [pltpu.VMEM(second_shape, F32), pltpu.VMEM(first_shape, F32)]
        return near + [pltpu.VMEM(first_shape, F32), pltpu.VMEM(second_shape, F32)] * 2

    rest = WIDTH - CUT
    half = SHARD // 2
    table_new, acc_new, down_step, up_step = pl.pallas_call(
        reduce_kernel,
        out_shape=(
            shaped((SHARD, EMB)), shaped((SHARD // 128, 128)),
            shaped((4, WIDTH)), shaped((4, WIDTH)),
        ),
        in_specs=[ANY] * 3 + [VMEM] * 3,
        out_specs=(VMEM,) * 4,
        scratch_shapes=[
            pltpu.VMEM((SHARD, EMB), F32), pltpu.VMEM((SHARD, EMB), F32),
            pltpu.VMEM((half, EMB), F32), pltpu.VMEM((half, EMB), F32),
            pltpu.VMEM((4, 4, 32, WIDTH), F32),
        ]
        + ring_buffers((half, EMB), (half, EMB))
        + ring_buffers((4, 32, 896), (4, 32, 896))
        + ring_buffers((4, 32, 896), (4, 32, 768))
        + ring_buffers((32, 896), (32, 896))
        + ring_buffers((32, 896), (32, 768))
        + ring_buffers((8, CUT), (8, rest))
        + [
            pltpu.VMEM((4, 32, CUT), F32), pltpu.VMEM((4, 32, rest), F32),
            pltpu.VMEM((32, CUT), F32), pltpu.VMEM((32, rest), F32),
            DMA((2, 2 + 4 * CHUNKS)), DMA((5, 2, 6)), DMA((5,)),
        ],
        compiler_params=params(50, collective_id=1, has_side_effects=True),
        name="reduce_update",
    )(
        tables.reshape(LOCALS, SHARD, EMB), dense.reshape(4, 4, 32, WIDTH), table_store,
        table_acc.reshape(-1, 128), down_acc, up_acc,
    )
    small_new, small_acc_new = pl.pallas_call(
        small_kernel,
        out_shape=(shaped((TR * RS, EMB)), shaped((TR * RS // 128, 128))),
        in_specs=[VMEM] * 3,
        out_specs=(VMEM,) * 2,
        compiler_params=params(16),
        name="small_update",
    )(small_store, small_acc.reshape(-1, 128), small_total)
    return (
        table_new, acc_new.reshape(-1), small_new, small_acc_new.reshape(-1), down_step, up_step,
    )


def solution(mesh):
    both = ("hst", "local")
    rows = P(both, None)
    return jax.shard_map(
        on_device,
        mesh=mesh,
        in_specs=(
            rows, P(both), P(), P(), P(), P(), P(), P(), P(both, None, None), P(both, None, None),
            rows, P(both), P(), P(), rows, rows,
        ),
        out_specs=(rows, P(both), P(), P(), rows, rows),
        check_vma=False,
    )
```

time: 576 us -> 235 us (0.41)
  matrix products: 340 us -> 0 us
  Pallas kernels: 0 us -> 169 us
  waiting for transfers between devices: 89 us -> 32.6 us
  local copies, waits for them, and re-layouts: 65.9 us -> 17 us
  loops' own time: 26.7 us -> 0 us
  other arithmetic: 18.3 us -> 0.8 us
  starting transfers between devices: 16.3 us -> 0.04 us
    dot_general x48 -> x0, matrix products: 340 us -> none  [the longest x40 322 us: one_block(): return jnp.dot(counts, grads, precision=lax.Precision.HIGHEST)]
    pallas_call x0 -> x5, Pallas kernels: none -> 169 us  [the longest x1 84 us: on_device(): pl.pallas_call(reduce_kernel, out_shape=(shaped((SHARD, EMB)), shaped((SH...]
    reduce_scatter x1 -> x0, waiting for transfers between devices: 70.4 us -> none  [on_device(): lax.psum_scatter(host_grad, 'local', scatter_dimension=0, tiled=True)]
    slice x36 -> x0, local copies, waits for them, and re-layouts: 35.1 us -> none  [the longest x32 33.8 us: one_block(): row_ids[None, :, pooled] == wanted[:, None]]
    psum x1, waiting for transfers between devices: 0.02 us -> 32.6 us  [on_device(): small_total = lax.psum(small_sum, ('hst', 'local'))]
    another operation x5 -> x0, loops' own time: 26.7 us -> none  [pooled_rows(): blocks = lax.map(one_block, jnp.arange(block_count, dtype=jnp.int32))]
    dynamic_slice x40 -> x0, local copies, waits for them, and re-layouts: 23.5 us -> none  [pooled_rows(): blocks = lax.map(one_block, jnp.arange(block_count, dtype=jnp.int32))]
    all_to_all x2 -> x0, waiting for transfers between devices: 18.6 us -> none  [the longest x1 18.6 us: on_device(): lax.all_to_all(send_grads, 'hst', split_axis=0, concat_axis=0, tiled=True)]
  transfers between devices with their start and end apart: 4 -> 1, of which waited for: 2 -> 1; matrix products, arithmetic and copies ran while one was open for 72% -> 0% of each run, Pallas kernels for 0% -> 49%
where the time goes in v2:
time: 235 us; the launch traced here: 234 us
  Pallas kernels  169 us (72%)
  waiting for transfers between devices  32.6 us (14%)
  local copies, waits for them, and re-layouts  17 us (7%)
  between operations  14.8 us (6%)
    pallas_call x1, Pallas kernels, on_device(): pl.pallas_call(reduce_kernel, out_shape=(shaped((SHARD, EMB)), shaped((SH...  84 us
    pallas_call x1, Pallas kernels, on_device(): pl.pallas_call(exchange_kernel, out_shape=(shaped((HOSTS, PACK, EMB)), sh...  43.4 us
    psum x1, waiting for transfers between devices, on_device(): small_total = lax.psum(small_sum, ('hst', 'local'))  32.6 us
    pallas_call x1, Pallas kernels, on_device(): pl.pallas_call(pooled_kernel, out_shape=shaped((LOCALS * SHARD, EMB)), in...  30.9 us
    unnamed x36, local copies, waits for them, and re-layouts  15.6 us
    pallas_call x1, Pallas kernels, on_device(): pl.pallas_call(dense_kernel, out_shape=(shaped((HOSTS, PACK, EMB)), shape...  5.61 us
    pallas_call x1, Pallas kernels, on_device(): pl.pallas_call(small_kernel, out_shape=(shaped((TR * RS, EMB)), shaped((T...  5.13 us
  transfers between devices with their start and end apart: 1, of which 1 were waited for; matrix products, arithmetic and copies ran while one was open for 0% of the time, Pallas kernels for 49%

profile of v2, /device:TPU:0, one launch (start us, length us, event | category | flops | bytes accessed | tf_op | source)
XLA Modules:
  0.0 234.3 jit_solution(1009716716515717205)
XLA Ops:
  7.2 0.0 all-reduce.3.cloned.1.call-start
  7.2 0.8 convert_bitcast_fusion
  8.0 0.7 reshape.43.bias
  8.7 0.7 reshape.44.head
  10.1 0.0 copy-start
  10.2 2.0 copy-done
  12.1 0.0 copy-start.1
  12.1 2.0 copy-done.1
  14.1 0.0 copy-start.8
  14.1 1.2 copy-done.8
  15.3 0.0 copy-start.14
  15.3 0.7 copy-done.14
  16.0 0.0 copy-start.15
  16.0 0.7 copy-done.15
  16.6 0.0 copy-start.13
  16.6 5.6 %dense_backward.1 = (f32[32,136,128]{2,1,0:T(8,128)S(1)}, f32[128,512]{1,0:T(8,128)S(1)}, bf16[256,3456]{1,0:T(8,128)(2,1)S(1)}, bf16[256,512]{1,0:T(8,128)(2,1)S(1)}) custom-call(bf16[128,3456]{1,0:T(8,128)(2,1)S(1)} %copy-done.8, s32[1,128]{1,0:T(1,128)S(1)} %bitcast.16, f32[1,3456]{1,0:T(1,128)S(1)} %reshape.43.bias, f32[1,3456]{1,0:T(1,128)S(1)} %reshape.44.head, ...), custom_call_target="tpu_custom_call" | custom-call | tf_op jit(solution)/shard_map/dense_backward/pallas_call | solution.py:534
  22.2 0.0 copy-start.3
  22.3 1.4 copy-done.3
  23.6 0.0 copy-done.13
  23.6 43.4 %exchange.1 = (f32[32,136,128]{2,1,0:T(8,128)}, s32[128,128]{1,0:T(8,128)S(1)}, f32[512,3456]{1,0:T(8,128)}, f32[4096,128]{1,0:T(8,128)}) custom-call(f32[32,136,128]{2,1,0:T(8,128)} %copy-done.3, bf16[256,3456]{1,0:T(8,128)(2,1)S(1)} %get-tuple-element.21.rights, bf16[256,512]{1,0:T(8,128)(2,1)S(1)} %get-tuple-element.22.lows, ...), custom_call_target="tpu_custom_call" | custom-call | tf_op jit(solution)/shard_map/exchange/pallas_call | solution.py:553
  67.0 0.0 all-reduce.3.cloned.1.call-update
  67.0 0.0 copy-start.2
  67.0 1.6 copy-done.2
  68.6 0.0 copy-start.9
  68.6 0.0 copy-start.10
  68.6 0.0 copy-start.12
  68.7 30.9 %pooled_rows.1 = f32[16384,128]{1,0:T(8,128)} custom-call(s32[16384]{0:T(1024)S(1)} %bitcast.11, f32[32,136,128]{2,1,0:T(8,128)S(1)} %copy-done.2), custom_call_target="tpu_custom_call" | custom-call | tf_op jit(solution)/shard_map/pooled_rows/pallas_call | solution.py:571
  99.5 0.0 copy-done.9
  99.5 0.0 copy-done.10
  99.5 0.0 copy-done.12
  99.6 0.0 copy-start.4
  99.6 0.0 copy-start.11
  99.6 84.0 %reduce_update.1 = (f32[4096,128]{1,0:T(8,128)S(1)}, f32[32,128]{1,0:T(8,128)S(1)}, f32[4,3456]{1,0:T(4,128)S(1)}, f32[4,3456]{1,0:T(4,128)S(1)}) custom-call(f32[4,4096,128]{2,1,0:T(8,128)} %bitcast.17, f32[4,4,32,3456]{3,2,1,0:T(8,128)} %bitcast.18, f32[4096,128]{1,0:T(8,128)} %store_hbm.1, f32[32,128]{1,0:T(8,128)S(1)} %bitcast.14, ...), custom_call_target="tpu_custom_call" | custom-call | tf_op jit(solution)/shard_map/reduce_update/pallas_call | solution.py:587
  183.6 0.0 copy-start.6
  183.6 1.3 copy-done.6
  184.9 32.6 %all-reduce.3.cloned.1.call-done.grads = f32[4096,128]{1,0:T(8,128)} async-done(((f32[4096,128]{1,0:T(8,128)}), f32[4096,128]{1,0:T(8,128)}) %all-reduce.3.cloned.1.call-update) | async-done | bytes 2097168 | tf_op jit(solution)/shard_map/psum | solution.py:570
  217.5 0.0 copy-done.4
  217.5 0.0 copy-done.11
  217.5 0.0 copy-start.5
  217.5 1.6 copy-done.5
  219.1 0.0 copy-start.7
  219.1 5.1 %small_update.1 = (f32[4096,128]{1,0:T(8,128)}, f32[32,128]{1,0:T(8,128)}) custom-call(f32[4096,128]{1,0:T(8,128)S(1)} %copy-done.4, f32[32,128]{1,0:T(8,128)S(1)} %bitcast.12, f32[4096,128]{1,0:T(8,128)S(1)} %copy-done.5), custom_call_target="tpu_custom_call" | custom-call | tf_op jit(solution)/shard_map/small_update/pallas_call | solution.py:617
  224.2 0.0 copy-done.7
  224.2 1.3 copy.28
  225.6 0.6 copy.29
  226.2 0.6 copy.30
  226.8 0.6 copy.31
  (1 shorter events, 0.0 us)
Async XLA Ops:
  7.2 210.3 %all-reduce.3.cloned.1.call-start = ((), (), s32[]{:S(2)}) async-start(), calls=%async_computation | async-start | bytes 4194304 | tf_op jit(solution)/shard_map/psum | solution.py:570
  10.1 2.0 copy-start
  12.1 2.0 copy-start.1
  14.1 1.2 copy-start.8
  15.3 0.7 copy-start.14
  16.0 0.7 copy-start.15
  16.6 7.0 %copy-start.13 = (s32[128,4,4]{0,2,1:T(4,128)S(1)}, s32[128,4,4]{0,2,1:T(4,128)}, u32[]{:S(2)}) copy-start(s32[128,4,4]{0,2,1:T(4,128)} %param.25) | copy-start | bytes 24580
  22.2 1.4 copy-start.3
  67.0 1.6 copy-start.2
  68.6 30.9 %copy-start.9 = (f32[4,3456]{1,0:T(4,128)S(1)}, f32[4,3456]{1,0:T(4,128)}, u32[]{:S(2)}) copy-start(f32[4,3456]{1,0:T(4,128)} %down_acc.1) | copy-start | bytes 165892
  68.6 30.9 %copy-start.10 = (f32[4,3456]{1,0:T(4,128)S(1)}, f32[4,3456]{1,0:T(4,128)}, u32[]{:S(2)}) copy-start(f32[4,3456]{1,0:T(4,128)} %up_acc.1) | copy-start | bytes 165892
  68.6 30.9 %copy-start.12 = (f32[4096]{0:T(1024)S(1)}, f32[4096]{0:T(1024)}, u32[]{:S(2)}) copy-start(f32[4096]{0:T(1024)} %param.27) | copy-start | bytes 49156
  99.6 117.9 %copy-start.4 = (f32[4096,128]{1,0:T(8,128)S(1)}, f32[4096,128]{1,0:T(8,128)}, u32[]{:S(2)}) copy-start(f32[4096,128]{1,0:T(8,128)} %store.1) | copy-start | bytes 6291460
  99.6 117.9 %copy-start.11 = (f32[4096]{0:T(1024)S(1)}, f32[4096]{0:T(1024)}, u32[]{:S(2)}) copy-start(f32[4096]{0:T(1024)} %param.29) | copy-start | bytes 49156
  183.6 1.3 copy-start.6
  217.5 1.6 copy-start.5
  219.1 5.1 %copy-start.7 = (f32[4096,128]{1,0:T(8,128)S(1)}, f32[4096,128]{1,0:T(8,128)}, u32[]{:S(2)}) copy-start(f32[4096,128]{1,0:T(8,128)} %copy-done.6) | copy-start | bytes 6291460
Sparse Core Ops, SparseCore 0:
  67.1 150.3 all-reduce.2

commit v3 on v2

v3 whole, which is shorter than its diff:
```python
import functools

import jax
import jax.numpy as jnp
from jax import lax
from jax.experimental import pallas as pl
from jax.experimental.pallas import tpu as pltpu
from jax.sharding import PartitionSpec as P

TS = 22
TR = 4
RS = 1024
HOT = 4
SHARD = 4096
EMB = 128
RANK = 512
WIDTH = 3456
HOSTS = 32
LOCALS = 4
SAMPLES = 128
PACK = SAMPLES + 8
FULL = WIDTH + TR * EMB
CUT = 2048
TIES = ((2, 0), (2, 1), (2, 3), (0, 2), (1, 2), (3, 2), (2, 2))
STRAIGHT = ((0, 1), (0, 3), (1, 0), (3, 0), (1, 1), (1, 3), (3, 1), (3, 3))
LEARN_RATE = 0.05
MESH = pl.DeviceIdType.MESH
F32 = jnp.float32
BF16 = jnp.bfloat16


def product(left, right, left_dim=1, right_dim=0):
    return lax.dot_general(
        left, right, (((left_dim,), (right_dim,)), ((), ())), preferred_element_type=F32
    )


def diagonal():
    return lax.broadcasted_iota(jnp.int32, (128, 128), 0) == lax.broadcasted_iota(
        jnp.int32, (128, 128), 1
    )


def dense_kernel(
    labels, bias, head, head_bias, place, bags, features_hbm, down_hbm, up_hbm,
    send, small, rights, lows, down, up, cross, sems,
):
    features = rights.at[0:SAMPLES]
    features_copy = pltpu.make_async_copy(features_hbm, features, sems.at[2])
    down_copy = pltpu.make_async_copy(down_hbm, down, sems.at[0])
    up_copy = pltpu.make_async_copy(up_hbm, up, sems.at[1])
    features_copy.start()
    down_copy.start()
    up_copy.start()

    @pl.loop(0, HOSTS)
    def _(slot):
        send[slot] = jnp.zeros((PACK, EMB), F32)

    parts = [(start, min(256, WIDTH - start)) for start in range(0, WIDTH, 256)]

    def tiles(ref, start, width):
        rows = [ref[t : t + 1, :] for t in range(start // 128, (start + width) // 128)]
        return jnp.concatenate(rows, axis=1)

    features_copy.wait()
    down_copy.wait()
    low_proj = product(features[...], down[...], 1, 1).astype(BF16)
    lows[SAMPLES:, :] = low_proj
    up_copy.wait()
    terms = jnp.zeros((SAMPLES, 128), F32)
    for start, width in parts:
        at = pl.ds(start, width)
        out = product(low_proj, up[:, at]) + tiles(bias, start, width)
        cross[:, at] = out
        wide = features[:, at].astype(F32)
        weighted = (wide * out + wide) * tiles(head, start, width)
        for tile in range(width // 128):
            terms = terms + weighted[:, tile * 128 : (tile + 1) * 128]
    logit = jnp.sum(terms, axis=1, keepdims=True) + head_bias[0]
    label = jnp.sum(
        jnp.where(diagonal(), labels[...].astype(F32), 0.0), axis=1, keepdims=True
    )
    logit_grad = jax.nn.sigmoid(logit) - label
    for start, width in parts:
        at = pl.ds(start, width)
        layer_grad = logit_grad * tiles(head, start, width)
        rights[SAMPLES:, at] = (layer_grad * features[:, at].astype(F32)).astype(BF16)
    low_grad = product(rights[SAMPLES:, :], up[...], 1, 1).astype(BF16)
    lows[0:SAMPLES, :] = low_grad
    for start, width in parts:
        at = pl.ds(start, width)
        layer_grad = logit_grad * tiles(head, start, width)
        grad = layer_grad * (cross[:, at] + 1.0) + product(low_grad, down[:, at])
        for tile in range(width // 128):
            piece = grad[:, tile * 128 : (tile + 1) * 128]
            table = start // 128 + tile - 1
            if 0 <= table < TS:
                slot = place[table]
                send[slot, 0:SAMPLES, :] = piece
                send[slot, SAMPLES : SAMPLES + HOT, :] = bags[table].astype(F32)
            elif table >= TS:
                small[:, (table - TS) * EMB : (table - TS + 1) * EMB] = piece


def exchange_kernel(
    send, rights_hbm, lows_hbm, small_hbm, small_ids,
    got_hbm, ids, dense,
    rights, lows, small, got, left_own, left_other, own, other, arrived, split, relayed,
    sems, relay_sems, core_sems, out_sems, in_sems, own_sem,
):
    host = lax.axis_index("hst")
    core = lax.rem(host, 2)
    z, y = host // 8, (host // 2) % 4
    partner = host + 1 - 2 * core
    operands = [
        pltpu.make_async_copy(source, target, in_sems.at[i])
        for i, (source, target) in enumerate(
            ((lows_hbm, lows), (rights_hbm, rights), (small_hbm, small))
        )
    ]
    for copy in operands:
        copy.start()
    barrier = pltpu.get_barrier_semaphore()

    @pl.loop(1, HOSTS)
    def _(off):
        pl.semaphore_signal(
            barrier, inc=1, device_id={"hst": lax.rem(host + off, HOSTS)}, device_id_type=MESH
        )

    def chip(dz, dy):
        return (lax.rem(z + dz + 4, 4) * 4 + lax.rem(y + dy + 4, 4)) * 2

    def bag_copy(src, to, slot, off, cores):
        at = (off[0] * 4 + off[1]) * 2
        return pltpu.make_async_remote_copy(
            src_ref=src,
            dst_ref=got.at[slot],
            send_sem=sems.at[0, at + cores[1]],
            recv_sem=sems.at[1, at + cores[0]],
            device_id={"hst": to},
            device_id_type=MESH,
        )

    def straight(off, target):
        to = chip(*off) + target
        return bag_copy(send.at[to], to, host, off, (core, target))

    turn = 1 - 2 * core

    def halfway(index):
        dz, dy = TIES[index]
        to = chip(turn if dz == 2 else 0, turn if dy == 2 else 0) + core
        return pltpu.make_async_remote_copy(
            src_ref=send.at[pl.ds(chip(dz, dy), 2)],
            dst_ref=relayed.at[index],
            send_sem=relay_sems.at[0, index],
            recv_sem=relay_sems.at[1, index],
            device_id={"hst": to},
            device_id_type=MESH,
        )

    def onward(index, target):
        dz, dy = TIES[index]
        to = chip(turn if dz == 2 else dz, turn if dy == 2 else dy) + target
        source = chip(-turn if dz == 2 else 0, -turn if dy == 2 else 0) + core
        return bag_copy(relayed.at[index, target], to, source, TIES[index], (core, target))

    def arrival(off, source_core):
        source = chip(-off[0], -off[1]) + source_core
        return bag_copy(send.at[source], source, source, off, (source_core, source_core))

    def neighbour():
        return pltpu.make_async_remote_copy(
            src_ref=send.at[partner],
            dst_ref=got.at[host],
            send_sem=sems.at[0, 0],
            recv_sem=sems.at[1, 0],
            device_id={"hst": partner},
            device_id_type=MESH,
        )

    def from_neighbour():
        return pltpu.make_async_remote_copy(
            src_ref=send.at[partner],
            dst_ref=got.at[partner],
            send_sem=sems.at[0, 0],
            recv_sem=sems.at[1, 0],
            device_id={"hst": partner},
            device_id_type=MESH,
        )

    pl.semaphore_wait(barrier, HOSTS - 1)
    for index in range(len(TIES)):
        halfway(index).start()
    for off in STRAIGHT:
        for target in range(2):
            straight(off, target).start()
    neighbour().start()
    mine = pltpu.make_async_copy(send.at[host], got.at[host], own_sem)
    mine.start()

    def spread(target, left):
        row = lax.broadcasted_iota(jnp.int32, (RANK, RANK), 0)
        rank = lax.broadcasted_iota(jnp.int32, (RANK, RANK), 1)
        place = row & 7
        base = ((row >> 5) * 2 + target) * 16 + ((row >> 3) & 3) * 4
        for part in range(2):
            want = jnp.where((place >> 2) == part, base + place - 4 * part, -1)
            chosen = jnp.where(want == rank, 1.0, 0.0).astype(BF16)
            left[:, part * SAMPLES : (part + 1) * SAMPLES] = product(
                chosen, lows[part * SAMPLES : (part + 1) * SAMPLES, :], 1, 1
            ).astype(BF16)

    def grads(left, out, group):
        @pl.loop(0, WIDTH // 384)
        def _(part):
            at = pl.ds(pl.multiple_of(part * 384, 384), 384)
            out[group * 128 : (group + 1) * 128, at] = product(
                left[group * 128 : (group + 1) * 128, :], rights[:, at]
            )

    for copy in operands:
        copy.wait()
    for table in range(TR):
        value = small[:, table * EMB : (table + 1) * EMB]
        high = value.astype(BF16)
        split[table, :, 0:EMB] = high
        split[table, :, EMB:] = (value - high.astype(F32)).astype(BF16)

    def small_sums(target, out, group):
        @pl.loop(0, 4)
        def _(part):
            block = (group * 4 + part) * 2 + target
            rows = (block % 8) * 128 + lax.broadcasted_iota(jnp.int32, (128, SAMPLES), 0)
            wanted = small_ids[group]
            counts = jnp.zeros((128, SAMPLES), F32)
            for k in range(HOT):
                counts = counts + jnp.where(rows == wanted[k : k + 1, :], 1.0, 0.0)
            both = product(counts.astype(BF16), split[group])
            total = both[:, 0:EMB] + both[:, EMB:]
            for x in range(LOCALS):
                at = pl.ds(pl.multiple_of((group * 4 + part) * 32 + x * 8, 8), 8)
                for tile in range(4):
                    start = x * 32 + tile * 8
                    lanes = pl.ds(WIDTH + tile * 128, 128)
                    out[at, lanes] = total[start : start + 8, :]

    def core_copy(group):
        rows = pl.ds(group * 128, 128)
        return pltpu.make_async_remote_copy(
            src_ref=other.at[rows],
            dst_ref=arrived.at[rows],
            send_sem=core_sems.at[0, group],
            recv_sem=core_sems.at[1, group],
            device_id={"hst": partner},
            device_id_type=MESH,
        )

    def out_copy(group):
        rows = pl.ds(group * 128, 128)
        return pltpu.make_async_copy(own.at[rows], dense.at[rows], out_sems.at[group])

    spread(1 - core, left_other)
    for group in range(4):
        grads(left_other, other, group)
        small_sums(1 - core, other, group)
        core_copy(group).start()
    for index in range(len(TIES)):
        halfway(index).wait_recv()
        for target in range(2):
            onward(index, target).start()
    spread(core, left_own)
    for group in range(4):
        grads(left_own, own, group)
        small_sums(core, own, group)
    for group in range(4):
        core_copy(group).wait_recv()

        @pl.loop(0, 4)
        def _(part):
            rows = pl.ds(pl.multiple_of(group * 128 + part * 32, 32), 32)
            own[rows, :] = own[rows, :] + arrived[rows, :]

        out_copy(group).start()

    mine.wait()
    from_neighbour().wait_recv()
    for off in STRAIGHT + TIES:
        for source_core in range(2):
            arrival(off, source_core).wait_recv()

    @pl.loop(0, HOSTS // 2)
    def _(pair):
        low = got[pair * 2, pl.ds(SAMPLES, 8), :]
        high = got[pair * 2 + 1, pl.ds(SAMPLES, 8), :]
        ids[pl.ds(pl.multiple_of(pair * 8, 8), 8), :] = jnp.concatenate(
            [low[0:HOT], high[0:HOT]], axis=0
        ).astype(jnp.int32)

    result = pltpu.make_async_copy(got, got_hbm, own_sem)
    result.start()
    neighbour().wait_send()
    for off in STRAIGHT:
        for target in range(2):
            straight(off, target).wait_send()
    for index in range(len(TIES)):
        halfway(index).wait_send()
        for target in range(2):
            onward(index, target).wait_send()
    for group in range(4):
        core_copy(group).wait_send()
        out_copy(group).wait()
    result.wait()


def pooled_kernel(ids, grads_hbm, out, grads, *scratch):
    sums, sem, in_sem = scratch[:HOT], scratch[HOT], scratch[HOT + 1]
    operand = pltpu.make_async_copy(grads_hbm, grads, in_sem)
    operand.start()
    row_total = out.shape[0]
    step = 256

    @pl.loop(0, row_total // step)
    def _(i):
        rows = pl.ds(pl.multiple_of(i * step, step), step)
        for total in sums:
            total[rows, :] = jnp.zeros((step, EMB), F32)

    operand.wait()

    @pl.loop(0, HOSTS)
    def _(source):
        @pl.loop(0, SAMPLES // 16)
        def _(group):
            for pair in range(8):
                sample = group * 16 + pair * 2
                first = grads[source, pl.ds(sample, 1), :]
                second = grads[source, pl.ds(sample + 1, 1), :]
                at = [
                    ids[(source * HOT + k % HOT) * SAMPLES + sample + k // HOT]
                    for k in range(2 * HOT)
                ]
                held = [sums[k % HOT][pl.ds(at[k], 1), :] for k in range(2 * HOT)]
                new = [held[k] + first for k in range(HOT)]
                for k in range(HOT):
                    new.append(jnp.where(at[k] == at[HOT + k], new[k], held[HOT + k]) + second)
                for k in range(2 * HOT):
                    sums[k % HOT][pl.ds(at[k], 1), :] = new[k]

    @pl.loop(0, row_total // step)
    def _(i):
        rows = pl.ds(pl.multiple_of(i * step, step), step)
        sums[0][rows, :] = (sums[0][rows, :] + sums[1][rows, :]) + (
            sums[2][rows, :] + sums[3][rows, :]
        )
        pltpu.make_async_copy(sums[0].at[rows], out.at[rows], sem.at[i]).start()

    @pl.loop(0, row_total // step)
    def _(i):
        rows = pl.ds(pl.multiple_of(i * step, step), step)
        pltpu.make_async_copy(sums[0].at[rows], out.at[rows], sem.at[i]).wait()


class Ring:
    def __init__(self, place, right, left, sent, held, near, passed, sums, sems, chunks=1):
        self.place, self.right, self.left = place, right, left
        self.sent, self.held, self.near, self.passed = sent, held, near, passed
        self.sums, self.sems, self.chunks = sums, sems, chunks

    def piece(self, ref, chunk):
        if self.chunks == 1:
            return ref
        rows = ref.shape[0] // self.chunks
        return ref.at[pl.ds(chunk * rows, rows)]

    def copy(self, src, dst, kind, side, chunk):
        index = (kind * 2 + side) * self.chunks + chunk
        return pltpu.make_async_remote_copy(
            src_ref=self.piece(src, chunk), dst_ref=self.piece(dst, chunk),
            send_sem=self.sems.at[0, index], recv_sem=self.sems.at[1, index],
            device_id=self.left if side else self.right, device_id_type=MESH,
        )

    def next(self, side):
        return lax.rem(self.place + (3 if side else 1), 4)

    def far(self, side, chunk=0):
        src = self.sent(lax.rem(self.place + 2, 4), side)
        return self.copy(src, self.passed[side], 0, side, chunk)

    def direct(self, side, chunk=0):
        return self.copy(self.sent(self.next(side), 1 - side), self.near[side], 1, side, chunk)

    def relay(self, side, chunk=0):
        return self.copy(self.passed[side], self.sums[side], 2, side, chunk)

    def start(self, chunk=0):
        for side in range(2):
            self.far(side, chunk).start()

    def middle(self, chunk=0):
        for side in range(2):
            self.far(side, chunk).wait_recv()
            add_into(
                self.piece(self.passed[side], chunk),
                self.piece(self.held(self.next(side), side), chunk),
            )
            self.relay(side, chunk).start()
            self.direct(side, chunk).start()

    def arrive(self, chunk=0):
        for side in range(2):
            self.relay(side, chunk).wait_recv()
            self.direct(side, chunk).wait_recv()

    def finish(self, outs):
        self.arrive()
        add_three(outs[0], self.held(self.place, 0), self.sums[0], self.near[1])
        add_three(outs[1], self.held(self.place, 1), self.near[0], self.sums[1])

    def drain(self):
        for chunk in range(self.chunks):
            for side in range(2):
                self.far(side, chunk).wait_send()
                self.direct(side, chunk).wait_send()
                self.relay(side, chunk).wait_send()


def blocks_of(shape):
    if len(shape) == 3:
        return shape[0], lambda ref, i: ref.at[i]
    rows = min(shape[0], 32 if shape[1] > 256 else 128)
    return shape[0] // rows, lambda ref, i: ref.at[pl.ds(pl.multiple_of(i * rows, rows), rows)]


def add_into(total, term):
    count, at = blocks_of(total.shape)

    @pl.loop(0, count)
    def _(i):
        at(total, i)[...] = at(total, i)[...] + at(term, i)[...]


def add_three(out, first, second, third):
    count, at = blocks_of(out.shape)

    @pl.loop(0, count)
    def _(i):
        at(out, i)[...] = at(first, i)[...] + at(second, i)[...] + at(third, i)[...]


CHUNKS = 8
AHEAD = 3


def reduce_kernel(
    tables, dense, store_hbm, small_hbm, acc, small_acc, down_acc, up_acc,
    table_new, acc_new, small_new, small_acc_new, down_step, up_step,
    store, small, gathered, mine, ahead, behind, grads,
    t_near0, t_near1, t_pass0, t_pass1, t_sum0, t_sum1,
    a_near0, a_near1, a_pass0, a_pass1, a_sum0, a_sum1,
    b_near0, b_near1, b_pass0, b_pass1, b_sum0, b_sum1,
    c_near0, c_near1, c_pass0, c_pass1, c_sum0, c_sum1,
    d_near0, d_near1, d_pass0, d_pass1, d_sum0, d_sum1,
    e_near0, e_near1, e_pass0, e_pass1, e_sum0, e_sum1,
    a_out, b_out, c_out, d_out,
    t_sems, r_sems, g_sems, local_sems,
):
    host = lax.axis_index("hst")
    x = lax.axis_index("local")
    z, y, core = host // 8, (host // 2) % 4, host % 2

    def on_z(step):
        return {"hst": (lax.rem(z + step, 4) * 4 + y) * 2 + core}

    def on_y(step):
        return {"hst": (z * 4 + lax.rem(y + step, 4)) * 2 + core}

    def on_x(step):
        return {"local": lax.rem(x + step, 4)}

    barrier = pltpu.get_barrier_semaphore()
    for neighbours in (on_x, on_y, on_z):
        for step in (1, 2, 3):
            pl.semaphore_signal(
                barrier, inc=1, device_id=neighbours(step), device_id_type=MESH
            )
    partner = {"hst": host + 1 - 2 * core}
    pl.semaphore_signal(barrier, inc=1, device_id=partner, device_id_type=MESH)
    half = SHARD // 2
    right, left = lax.rem(x + 1, 4), lax.rem(x + 3, 4)
    locals_ = [
        pltpu.make_async_copy(tables.at[right, pl.ds(0, half)], ahead, local_sems.at[0]),
        pltpu.make_async_copy(tables.at[left, pl.ds(half, half)], behind, local_sems.at[1]),
        pltpu.make_async_copy(dense, grads, local_sems.at[2]),
        pltpu.make_async_copy(tables.at[x], mine, local_sems.at[3]),
        pltpu.make_async_copy(store_hbm, store, local_sems.at[4]),
        pltpu.make_async_copy(small_hbm, small, local_sems.at[5]),
    ]
    for copy in locals_:
        copy.start()
    pl.semaphore_wait(barrier, 10)

    first = {0: pl.ds(0, 1024), 1: pl.ds(1024, 1024)}
    second = {0: pl.ds(CUT, 1024), 1: pl.ds(CUT + 1024, 896)}
    inner = {0: pl.ds(0, 1024), 1: pl.ds(1024, 896)}
    table_ring = Ring(
        x, on_x(1), on_x(3),
        lambda t, s: tables.at[t, pl.ds(s * half, half)],
        lambda t, s: behind if s else ahead,
        (t_near0, t_near1), (t_pass0, t_pass1), (t_sum0, t_sum1), t_sems, CHUNKS,
    )
    a_ring = Ring(
        z, on_z(1), on_z(3),
        lambda t, s: dense.at[t, :, :, first[s]],
        lambda t, s: grads.at[t, :, :, first[s]],
        (a_near0, a_near1), (a_pass0, a_pass1), (a_sum0, a_sum1), r_sems.at[0],
    )
    b_ring = Ring(
        y, on_y(1), on_y(3),
        lambda t, s: dense.at[:, t, :, second[s]],
        lambda t, s: grads.at[:, t, :, second[s]],
        (b_near0, b_near1), (b_pass0, b_pass1), (b_sum0, b_sum1), r_sems.at[1],
    )
    c_at = lambda t, s: a_out.at[t, :, first[s]]
    c_ring = Ring(
        y, on_y(1), on_y(3), c_at, c_at, (c_near0, c_near1), (c_pass0, c_pass1), (c_sum0, c_sum1), r_sems.at[2]
    )
    d_at = lambda t, s: b_out.at[t, :, inner[s]]
    d_ring = Ring(
        z, on_z(1), on_z(3), d_at, d_at, (d_near0, d_near1), (d_pass0, d_pass1), (d_sum0, d_sum1), r_sems.at[3]
    )
    e_at = lambda t, s: (d_out if s else c_out).at[pl.ds(pl.multiple_of(t * 8, 8), 8)]
    e_ring = Ring(
        x, on_x(1), on_x(3), e_at, e_at, (e_near0, e_near1), (e_pass0, e_pass1), (e_sum0, e_sum1), r_sems.at[4]
    )

    eye = diagonal()

    def update(block, grad, before, acc_before, after, acc_after):
        rows = pl.ds(pl.multiple_of(block * 128, 128), 128)
        at = pl.ds(block, 1)
        acc_here = jnp.sum(jnp.where(eye, acc_before[at, :], 0.0), axis=1, keepdims=True)
        total = acc_here + jnp.sum(grad * grad, axis=1, keepdims=True) * (1.0 / EMB)
        after[rows, :] = before[rows, :] - grad * (LEARN_RATE * lax.rsqrt(total))
        acc_after[at, :] = jnp.sum(jnp.where(eye, total, 0.0), axis=0, keepdims=True)

    def finish_dense(side, start, stop):
        near = (e_near1, e_near0)[side]
        at = pl.ds(start, stop - start)
        return e_ring.held(x, side)[:, at] + e_ring.sums[side][:, at] + near[:, at]

    halves = (pl.ds(0, 256), pl.ds(256, 256))

    def gather_copy(index, view, to):
        return pltpu.make_async_remote_copy(
            src_ref=view, dst_ref=view, send_sem=g_sems.at[0, index],
            recv_sem=g_sems.at[1, index], device_id=to, device_id_type=MESH,
        )

    def stage(number, back):
        copies = []
        for step in (1, 2, 3):
            there = lax.rem(4 - step, 4) if back else 0
            at_z, at_y, at_x = (lax.rem(place + there, 4) for place in (z, y, x))
            if number == 0:
                views = [(gathered.at[z, y, core, at_x], on_x)]
            elif number == 1:
                views = [
                    (gathered.at[z, at_y, core, :, :, halves[0]], on_y),
                    (gathered.at[at_z, y, core, :, :, halves[1]], on_z),
                ]
            else:
                views = [
                    (gathered.at[at_z, :, core, :, :, halves[0]], on_z),
                    (gathered.at[:, at_y, core, :, :, halves[1]], on_y),
                ]
            for view, axis in views:
                copies.append(gather_copy(number * 6 + len(copies), view, axis(step)))
        return copies

    def begin(number):
        for copy in stage(number, False):
            copy.start()

    def arrived(number):
        for copy in stage(number, True):
            copy.wait_recv()

    def pass_on(chunk):
        table_ring.middle(chunk)
        if chunk + AHEAD < CHUNKS:
            table_ring.start(chunk + AHEAD)

    rows_chunk = half // CHUNKS

    def update_tables(chunk):
        table_ring.arrive(chunk)
        for side in range(2):
            near = (t_near1, t_near0)[side]

            @pl.loop(0, rows_chunk // 128)
            def _(part):
                inside = pl.ds(pl.multiple_of(chunk * rows_chunk + part * 128, 128), 128)
                block = side * (half // 128) + chunk * (rows_chunk // 128) + part
                rows = pl.ds(pl.multiple_of(block * 128, 128), 128)
                grad = mine[rows, :] + table_ring.sums[side][inside, :] + near[inside, :]
                update(block, grad, store, acc, table_new, acc_new)

    a_ring.start()
    b_ring.start()
    for chunk in range(AHEAD):
        table_ring.start(chunk)
    for copy in locals_[:3]:
        copy.wait()
    pass_on(0)
    a_ring.middle()
    b_ring.middle()
    pass_on(1)
    pass_on(2)
    pass_on(3)
    for copy in locals_[3:]:
        copy.wait()
    a_ring.finish([a_out.at[:, :, first[s]] for s in range(2)])
    c_ring.start()
    b_ring.finish([b_out.at[:, :, inner[s]] for s in range(2)])
    d_ring.start()
    update_tables(0)
    pass_on(4)
    c_ring.middle()
    d_ring.middle()
    update_tables(1)
    c_ring.finish([c_out.at[:, first[s]] for s in range(2)])
    d_ring.finish([d_out.at[:, inner[s]] for s in range(2)])
    e_ring.start()
    pass_on(5)
    e_ring.middle()
    update_tables(2)
    e_ring.arrive()
    gathered[z, y, core, x] = finish_dense(1, WIDTH - CUT, FULL - CUT)
    begin(0)
    pass_on(6)
    for side, stop in ((0, CUT), (1, WIDTH - CUT)):
        total = finish_dense(side, 0, stop)
        at = pl.ds(side * CUT, stop)
        for step, before, rows in ((down_step, down_acc, 0), (up_step, up_acc, 4)):
            grad = total[rows : rows + 4]
            step[:, at] = grad * lax.rsqrt(before[:, at] + grad * grad)
    arrived(0)
    begin(1)
    update_tables(3)
    update_tables(4)
    arrived(1)
    begin(2)
    pass_on(7)
    update_tables(5)
    arrived(2)
    gather_copy(18, gathered.at[:, :, core], partner).start()
    update_tables(6)
    gather_copy(18, gathered.at[:, :, 1 - core], partner).wait_recv()

    @pl.loop(0, TR * RS // 128)
    def _(block):
        mixed = gathered.at[block // 8, (block // 2) % 4, block % 2]
        grad = jnp.concatenate(
            [
                mixed[place, :, tile * 128 : (tile + 1) * 128]
                for place in range(LOCALS)
                for tile in range(4)
            ],
            axis=0,
        )
        update(block, grad, small, small_acc, small_new, small_acc_new)

    update_tables(7)
    for ring in (table_ring, a_ring, b_ring, c_ring, d_ring, e_ring):
        ring.drain()
    for number in range(3):
        for copy in stage(number, False):
            copy.wait_send()
    gather_copy(18, gathered.at[:, :, core], partner).wait_send()


def shaped(shape, dtype=F32):
    return jax.ShapeDtypeStruct(shape, dtype)


HBM = pl.BlockSpec(memory_space=pltpu.HBM)
VMEM = pl.BlockSpec(memory_space=pltpu.VMEM)
SMEM = pl.BlockSpec(memory_space=pltpu.SMEM)
DMA = pltpu.SemaphoreType.DMA


def params(mebibytes, **others):
    return pltpu.CompilerParams(vmem_limit_bytes=mebibytes << 20, **others)


def on_device(
    features, labels, cross_down, cross_up, cross_bias, head_weight, head_bias, table_place,
    bag_rows, small_rows, table_store, table_acc, small_store, small_acc, down_acc, up_acc,
):
    bags = jnp.transpose(bag_rows, (1, 2, 0))
    small_ids = jnp.transpose(small_rows, (1, 2, 0))
    send, small, rights, lows = pl.pallas_call(
        dense_kernel,
        out_shape=(
            shaped((HOSTS, PACK, EMB)), shaped((SAMPLES, TR * EMB)),
            shaped((2 * SAMPLES, WIDTH), BF16), shaped((2 * SAMPLES, RANK), BF16),
        ),
        in_specs=[VMEM] * 3 + [SMEM] * 2 + [VMEM] + [HBM] * 3,
        out_specs=(VMEM,) * 4,
        scratch_shapes=[
            pltpu.VMEM((RANK, WIDTH), BF16), pltpu.VMEM((RANK, WIDTH), BF16),
            pltpu.VMEM((SAMPLES, WIDTH), F32), DMA((3,)),
        ],
        compiler_params=params(60),
        name="dense_backward",
    )(
        labels.reshape(1, -1), cross_bias.reshape(-1, 128), head_weight.reshape(-1, 128), head_bias,
        table_place, bags,
        features, cross_down, cross_up,
    )
    whole = (RANK, FULL)
    got, ids, dense = pl.pallas_call(
        exchange_kernel,
        out_shape=(
            shaped((HOSTS, PACK, EMB)), shaped((HOSTS * HOT, SAMPLES), jnp.int32), shaped(whole),
        ),
        in_specs=[HBM] * 4 + [VMEM],
        out_specs=(HBM, VMEM, HBM),
        scratch_shapes=[
            pltpu.VMEM((2 * SAMPLES, WIDTH), BF16), pltpu.VMEM((2 * SAMPLES, RANK), BF16),
            pltpu.VMEM((SAMPLES, TR * EMB), F32), pltpu.VMEM((HOSTS, PACK, EMB), F32),
            pltpu.VMEM((RANK, 2 * SAMPLES), BF16), pltpu.VMEM((RANK, 2 * SAMPLES), BF16),
            pltpu.VMEM(whole, F32), pltpu.VMEM(whole, F32), pltpu.VMEM(whole, F32),
            pltpu.VMEM((TR, SAMPLES, 2 * EMB), BF16),
            pltpu.VMEM((len(TIES), 2, PACK, EMB), F32),
            DMA((2, HOSTS)), DMA((2, len(TIES))), DMA((2, 4)), DMA((4,)), DMA((3,)), DMA,
        ],
        compiler_params=params(60, collective_id=0, has_side_effects=True),
        name="exchange",
    )(send, rights, lows, small, small_ids)
    tables = pl.pallas_call(
        pooled_kernel,
        out_shape=shaped((LOCALS * SHARD, EMB)),
        in_specs=[SMEM, HBM],
        out_specs=HBM,
        scratch_shapes=[pltpu.VMEM((HOSTS, PACK, EMB), F32)]
        + [pltpu.VMEM((LOCALS * SHARD, EMB), F32)] * HOT
        + [DMA((LOCALS * SHARD // 256,)), DMA],
        compiler_params=params(60),
        name="pooled_rows",
    )(ids.reshape(-1), got)

    def ring_buffers(first_shape, second_shape):
        near = [pltpu.VMEM(second_shape, F32), pltpu.VMEM(first_shape, F32)]
        return near + [pltpu.VMEM(first_shape, F32), pltpu.VMEM(second_shape, F32)] * 2

    rest = FULL - CUT
    half = SHARD // 2
    table_new, acc_new, small_new, small_acc_new, down_step, up_step = pl.pallas_call(
        reduce_kernel,
        out_shape=(
            shaped((SHARD, EMB)), shaped((SHARD // 128, 128)),
            shaped((TR * RS, EMB)), shaped((TR * RS // 128, 128)),
            shaped((4, WIDTH)), shaped((4, WIDTH)),
        ),
        in_specs=[HBM] * 4 + [VMEM] * 4,
        out_specs=(VMEM,) * 6,
        scratch_shapes=[
            pltpu.VMEM((SHARD, EMB), F32), pltpu.VMEM((TR * RS, EMB), F32),
            pltpu.VMEM((4, 4, 2, LOCALS, 8, TR * EMB), F32), pltpu.VMEM((SHARD, EMB), F32),
            pltpu.VMEM((half, EMB), F32), pltpu.VMEM((half, EMB), F32),
            pltpu.VMEM((4, 4, 32, FULL), F32),
        ]
        + ring_buffers((half, EMB), (half, EMB))
        + ring_buffers((4, 32, 1024), (4, 32, 1024))
        + ring_buffers((4, 32, 1024), (4, 32, 896))
        + ring_buffers((32, 1024), (32, 1024))
        + ring_buffers((32, 1024), (32, 896))
        + ring_buffers((8, CUT), (8, rest))
        + [
            pltpu.VMEM((4, 32, CUT), F32), pltpu.VMEM((4, 32, rest), F32),
            pltpu.VMEM((32, CUT), F32), pltpu.VMEM((32, rest), F32),
            DMA((2, 6 * CHUNKS)), DMA((5, 2, 6)), DMA((2, 19)), DMA((6,)),
        ],
        compiler_params=params(40, collective_id=1, has_side_effects=True),
        name="reduce_update",
    )(
        tables.reshape(LOCALS, SHARD, EMB), dense.reshape(4, 4, 32, FULL), table_store, small_store,
        table_acc.reshape(-1, 128), small_acc.reshape(-1, 128), down_acc, up_acc,
    )
    return (
        table_new, acc_new.reshape(-1), small_new, small_acc_new.reshape(-1), down_step, up_step,
    )


def solution(mesh):
    both = ("hst", "local")
    rows = P(both, None)
    return jax.shard_map(
        on_device,
        mesh=mesh,
        in_specs=(
            rows, P(both), P(), P(), P(), P(), P(), P(), P(both, None, None), P(both, None, None),
            rows, P(both), P(), P(), rows, rows,
        ),
        out_specs=(rows, P(both), P(), P(), rows, rows),
        check_vma=False,
    )
```

time: 235 us -> 182 us (0.77); the launches traced: 234 us -> 178 us
  waiting for transfers between devices: 32.6 us -> 0 us
  between operations: 14.8 us -> 1.4 us
  local copies, waits for them, and re-layouts: 17 us -> 6.71 us
    psum x1 -> x0, waiting for transfers between devices: 32.6 us -> none  [on_device(): small_total = lax.psum(small_sum, ('hst', 'local'))]
    pallas_call x1, Pallas kernels: 84 us -> 93.2 us  [on_device(): pl.pallas_call(reduce_kernel, out_shape=(shaped((SHARD, EMB)), shaped((SH...]
    unnamed x36 -> x18, local copies, waits for them, and re-layouts: 15.6 us -> 6.71 us
    pallas_call x1, Pallas kernels: 43.4 us -> 37.7 us  [on_device(): pl.pallas_call(exchange_kernel, out_shape=(shaped((HOSTS, PACK, EMB)), sh...]
    pallas_call x1 -> x0, Pallas kernels: 5.13 us -> none  [on_device(): pl.pallas_call(small_kernel, out_shape=(shaped((TR * RS, EMB)), shaped((T...]
    pallas_call x1, Pallas kernels: 5.61 us -> 9.25 us  [on_device(): pl.pallas_call(dense_kernel, out_shape=(shaped((HOSTS, PACK, EMB)), shape...]
  transfers between devices with their start and end apart: 1 -> 0, of which waited for: 1 -> 0; matrix products, arithmetic and copies ran while one was open for 0% -> 0% of each run, Pallas kernels for 49% -> 0%
where the time goes in v3:
time: 182 us; the launch traced here: 178 us
  Pallas kernels  170 us (93%)
  local copies, waits for them, and re-layouts  6.71 us (4%)
    pallas_call x1, Pallas kernels, on_device(): pl.pallas_call(reduce_kernel, out_shape=(shaped((SHARD, EMB)), shaped((SH...  93.2 us
    pallas_call x1, Pallas kernels, on_device(): pl.pallas_call(exchange_kernel, out_shape=(shaped((HOSTS, PACK, EMB)), sh...  37.7 us
    pallas_call x1, Pallas kernels, on_device(): pl.pallas_call(pooled_kernel, out_shape=shaped((LOCALS * SHARD, EMB)), in...  29.9 us
    pallas_call x1, Pallas kernels, on_device(): pl.pallas_call(dense_kernel, out_shape=(shaped((HOSTS, PACK, EMB)), shape...  9.25 us
    unnamed x18, local copies, waits for them, and re-layouts  6.71 us

profile of v3, /device:TPU:0, one launch (start us, length us, event | category | flops | bytes accessed | tf_op | source)
XLA Modules:
  0.0 178.2 jit_solution(2083321624712002786)
XLA Ops:
  1.3 9.3 %dense_backward.1 = (f32[32,136,128]{2,1,0:T(8,128)}, f32[128,512]{1,0:T(8,128)}, bf16[256,3456]{1,0:T(8,128)(2,1)}, bf16[256,512]{1,0:T(8,128)(2,1)}) custom-call(s32[1,128]{1,0:T(1,128)} %bitcast.23, f32[27,128]{1,0:T(8,128)} %bitcast.20, f32[27,128]{1,0:T(8,128)} %bitcast.21, f32[1]{0:T(128)S(6)} %copy.28.head_bias, s32[22]{0:T(128)} %place.1, ...), custom_call_target="tpu_custom_call" | custom-call | tf_op jit(solution)/shard_map/dense_backward/pallas_call | solution.py:706
  10.5 37.7 %exchange.1 = (f32[32,136,128]{2,1,0:T(8,128)}, s32[128,128]{1,0:T(8,128)}, f32[512,3968]{1,0:T(8,128)}) custom-call(f32[32,136,128]{2,1,0:T(8,128)} %get-tuple-element.19.send, bf16[256,3456]{1,0:T(8,128)(2,1)} %get-tuple-element.20.rights_hbm, bf16[256,512]{1,0:T(8,128)(2,1)} %get-tuple-element.21.lows_hbm, f32[128,512]{1,0:T(8,128)} %get-tuple-element.22.small_hbm, ...), custom_call_target="tpu_custom_call" | custom-call | tf_op jit(solution)/shard_map/exchange/pallas_call | solution.py:726
  48.3 0.0 copy-start
  48.3 0.0 copy-start.2
  48.3 0.0 copy-start.3
  48.3 0.0 copy-start.4
  48.3 0.0 copy-start.5
  48.3 29.9 %pooled_rows.1 = f32[16384,128]{1,0:T(8,128)} custom-call(s32[16384]{0:T(1024)} %bitcast.18, f32[32,136,128]{2,1,0:T(8,128)} %get-tuple-element.24.grads_hbm), custom_call_target="tpu_custom_call" | custom-call | tf_op jit(solution)/shard_map/pooled_rows/pallas_call | solution.py:745
  78.2 0.0 copy-done
  78.2 0.0 copy-done.2
  78.2 0.0 copy-done.3
  78.2 0.0 copy-done.4
  78.3 0.0 copy-done.5
  78.3 0.0 copy-start.1
  78.3 1.6 copy-done.1
  79.9 93.2 %reduce_update.1 = (f32[4096,128]{1,0:T(8,128)S(1)}, f32[32,128]{1,0:T(8,128)S(1)}, f32[4096,128]{1,0:T(8,128)S(1)}, f32[32,128]{1,0:T(8,128)S(1)}, f32[4,3456]{1,0:T(4,128)S(1)}, /*index=5*/f32[4,3456]{1,0:T(4,128)S(1)}) custom-call(f32[4,4096,128]{2,1,0:T(8,128)} %bitcast.16, f32[4,4,32,3968]{3,2,1,0:T(8,128)} %bitcast.17, f32[4096,128]{1,0:T(8,128)S(1)} %copy-done, ...), custom_call_target="tpu_custom_call" | custom-call | tf_op jit(solution)/shard_map/reduce_update/pallas_call | solution.py:763
  173.1 1.3 copy.29
  174.4 0.6 copy.30
  175.0 1.3 copy.31
  176.3 0.6 copy.32
  176.9 0.6 copy.33
  177.6 0.6 copy.34
Async XLA Ops:
  48.3 29.9 %copy-start = (f32[4096,128]{1,0:T(8,128)S(1)}, f32[4096,128]{1,0:T(8,128)}, u32[]{:S(2)}) copy-start(f32[4096,128]{1,0:T(8,128)} %store_hbm.1) | copy-start | bytes 6291460
  48.3 29.9 %copy-start.2 = (f32[4,3456]{1,0:T(4,128)S(1)}, f32[4,3456]{1,0:T(4,128)}, u32[]{:S(2)}) copy-start(f32[4,3456]{1,0:T(4,128)} %down_acc.1) | copy-start | bytes 165892
  48.3 29.9 %copy-start.3 = (f32[4,3456]{1,0:T(4,128)S(1)}, f32[4,3456]{1,0:T(4,128)}, u32[]{:S(2)}) copy-start(f32[4,3456]{1,0:T(4,128)} %up_acc.1) | copy-start | bytes 165892
  48.3 29.9 %copy-start.4 = (f32[4096]{0:T(1024)S(1)}, f32[4096]{0:T(1024)}, u32[]{:S(2)}) copy-start(f32[4096]{0:T(1024)} %param.27) | copy-start | bytes 49156
  48.3 29.9 %copy-start.5 = (f32[4096]{0:T(1024)S(1)}, f32[4096]{0:T(1024)}, u32[]{:S(2)}) copy-start(f32[4096]{0:T(1024)} %param.29) | copy-start | bytes 49156
  78.3 1.6 copy-start.1

commit v4 on v3

--- a/solution.py
+++ b/solution.py
@@ -19,8 +19,8 @@
 LOCALS = 4
 SAMPLES = 128
 PACK = SAMPLES + 8
-FULL = WIDTH + TR * EMB
-CUT = 2048
+FULL = WIDTH + EMB
+CUT = 1792
 TIES = ((2, 0), (2, 1), (2, 3), (0, 2), (1, 2), (3, 2), (2, 2))
 STRAIGHT = ((0, 1), (0, 3), (1, 0), (3, 0), (1, 1), (1, 3), (3, 1), (3, 3))
 LEARN_RATE = 0.05
@@ -42,7 +42,7 @@
 
 
 def dense_kernel(
-    labels, bias, head, head_bias, place, bags, features_hbm, down_hbm, up_hbm,
+    labels, bias, head, head_bias, place, bags, small_ids, features_hbm, down_hbm, up_hbm,
     send, small, rights, lows, down, up, cross, sems,
 ):
     features = rights.at[0:SAMPLES]
@@ -56,6 +56,10 @@
     @pl.loop(0, HOSTS)
     def _(slot):
         send[slot] = jnp.zeros((PACK, EMB), F32)
+
+    for table in range(TR):
+        small[table, SAMPLES:, :] = jnp.zeros((PACK - SAMPLES, EMB), F32)
+        small[table, SAMPLES : SAMPLES + HOT, :] = small_ids[table].astype(F32)
 
     parts = [(start, min(256, WIDTH - start)) for start in range(0, WIDTH, 256)]
 
@@ -100,23 +104,24 @@
                 send[slot, 0:SAMPLES, :] = piece
                 send[slot, SAMPLES : SAMPLES + HOT, :] = bags[table].astype(F32)
             elif table >= TS:
-                small[:, (table - TS) * EMB : (table - TS + 1) * EMB] = piece
+                small[table - TS, 0:SAMPLES, :] = piece
 
 
 def exchange_kernel(
-    send, rights_hbm, lows_hbm, small_hbm, small_ids,
+    send, rights_hbm, lows_hbm, small_hbm,
     got_hbm, ids, dense,
     rights, lows, small, got, left_own, left_other, own, other, arrived, split, relayed,
-    sems, relay_sems, core_sems, out_sems, in_sems, own_sem,
+    sems, relay_sems, core_sems, small_sems, out_sems, in_sems, own_sem,
 ):
     host = lax.axis_index("hst")
     core = lax.rem(host, 2)
     z, y = host // 8, (host // 2) % 4
+    x = lax.axis_index("local")
     partner = host + 1 - 2 * core
     operands = [
         pltpu.make_async_copy(source, target, in_sems.at[i])
         for i, (source, target) in enumerate(
-            ((lows_hbm, lows), (rights_hbm, rights), (small_hbm, small))
+            ((lows_hbm, lows), (rights_hbm, rights), (small_hbm.at[x], small.at[x]))
         )
     ]
     for copy in operands:
@@ -191,7 +196,25 @@
             device_id_type=MESH,
         )
 
-    pl.semaphore_wait(barrier, HOSTS - 1)
+    for step in (1, 2, 3):
+        pl.semaphore_signal(
+            barrier, inc=1, device_id={"local": lax.rem(x + step, 4)}, device_id_type=MESH
+        )
+
+    def small_copy(step, slot):
+        to = lax.rem(x + step, 4)
+        return pltpu.make_async_remote_copy(
+            src_ref=small_hbm.at[to],
+            dst_ref=small.at[slot],
+            send_sem=small_sems.at[0, step],
+            recv_sem=small_sems.at[1, step],
+            device_id={"local": to},
+            device_id_type=MESH,
+        )
+
+    pl.semaphore_wait(barrier, HOSTS + 2)
+    for step in (1, 2, 3):
+        small_copy(step, x).start()
     for index in range(len(TIES)):
         halfway(index).start()
     for off in STRAIGHT:
@@ -223,29 +246,31 @@
 
     for copy in operands:
         copy.wait()
-    for table in range(TR):
-        value = small[:, table * EMB : (table + 1) * EMB]
+    for step in (1, 2, 3):
+        small_copy(step, lax.rem(x - step + 4, 4)).wait_recv()
+
+    @pl.loop(0, LOCALS)
+    def _(source):
+        value = small[source, pl.ds(0, SAMPLES), :]
         high = value.astype(BF16)
-        split[table, :, 0:EMB] = high
-        split[table, :, EMB:] = (value - high.astype(F32)).astype(BF16)
+        split[source, :, 0:EMB] = high
+        split[source, :, EMB:] = (value - high.astype(F32)).astype(BF16)
 
     def small_sums(target, out, group):
-        @pl.loop(0, 4)
-        def _(part):
-            block = (group * 4 + part) * 2 + target
-            rows = (block % 8) * 128 + lax.broadcasted_iota(jnp.int32, (128, SAMPLES), 0)
-            wanted = small_ids[group]
+        spot = group * 128 + lax.broadcasted_iota(jnp.int32, (128, SAMPLES), 0)
+        row = ((spot >> 5) * 64 + target * 32 + (spot & 31)).astype(F32)
+        here = pl.ds(group * 128, 128)
+        lanes = pl.ds(WIDTH, EMB)
+        out[here, lanes] = jnp.zeros((128, EMB), F32)
+
+        @pl.loop(0, LOCALS)
+        def _(source):
+            wanted = small[source, pl.ds(SAMPLES, 8), :]
             counts = jnp.zeros((128, SAMPLES), F32)
             for k in range(HOT):
-                counts = counts + jnp.where(rows == wanted[k : k + 1, :], 1.0, 0.0)
-            both = product(counts.astype(BF16), split[group])
-            total = both[:, 0:EMB] + both[:, EMB:]
-            for x in range(LOCALS):
-                at = pl.ds(pl.multiple_of((group * 4 + part) * 32 + x * 8, 8), 8)
-                for tile in range(4):
-                    start = x * 32 + tile * 8
-                    lanes = pl.ds(WIDTH + tile * 128, 128)
-                    out[at, lanes] = total[start : start + 8, :]
+                counts = counts + jnp.where(row == wanted[k : k + 1, :], 1.0, 0.0)
+            both = product(counts.astype(BF16), split[source])
+            out[here, lanes] = out[here, lanes] + (both[:, 0:EMB] + both[:, EMB:])
 
     def core_copy(group):
         rows = pl.ds(group * 128, 128)
@@ -302,6 +327,8 @@
     result = pltpu.make_async_copy(got, got_hbm, own_sem)
     result.start()
     neighbour().wait_send()
+    for step in (1, 2, 3):
+        small_copy(step, x).wait_send()
     for off in STRAIGHT:
         for target in range(2):
             straight(off, target).wait_send()
@@ -400,6 +427,10 @@
         for side in range(2):
             self.far(side, chunk).start()
 
+    def start_direct(self, chunk=0):
+        for side in range(2):
+            self.direct(side, chunk).start()
+
     def middle(self, chunk=0):
         for side in range(2):
             self.far(side, chunk).wait_recv()
@@ -408,7 +439,6 @@
                 self.piece(self.held(self.next(side), side), chunk),
             )
             self.relay(side, chunk).start()
-            self.direct(side, chunk).start()
 
     def arrive(self, chunk=0):
         for side in range(2):
@@ -452,7 +482,6 @@
 
 
 CHUNKS = 8
-AHEAD = 3
 
 
 def reduce_kernel(
@@ -465,7 +494,9 @@
     c_near0, c_near1, c_pass0, c_pass1, c_sum0, c_sum1,
     d_near0, d_near1, d_pass0, d_pass1, d_sum0, d_sum1,
     e_near0, e_near1, e_pass0, e_pass1, e_sum0, e_sum1,
-    a_out, b_out, c_out, d_out,
+    u_near0, u_near1, u_pass0, u_pass1, u_sum0, u_sum1,
+    v_near0, v_near1, v_pass0, v_pass1, v_sum0, v_sum1,
+    a_out, b_out, c_out, d_out, u_out,
     t_sems, r_sems, g_sems, local_sems,
 ):
     host = lax.axis_index("hst")
@@ -503,9 +534,12 @@
         copy.start()
     pl.semaphore_wait(barrier, 10)
 
-    first = {0: pl.ds(0, 1024), 1: pl.ds(1024, 1024)}
-    second = {0: pl.ds(CUT, 1024), 1: pl.ds(CUT + 1024, 896)}
-    inner = {0: pl.ds(0, 1024), 1: pl.ds(1024, 896)}
+    first = {0: pl.ds(0, 896), 1: pl.ds(896, 896)}
+    second = {0: pl.ds(CUT, 896), 1: pl.ds(CUT + 896, 768)}
+    inner = {0: pl.ds(0, 896), 1: pl.ds(896, 768)}
+    third = pl.ds(WIDTH, EMB)
+    pairs = (pl.ds(0, 2), pl.ds(2, 2))
+    halves = (pl.ds(0, 16), pl.ds(16, 16))
     table_ring = Ring(
         x, on_x(1), on_x(3),
         lambda t, s: tables.at[t, pl.ds(s * half, half)],
@@ -531,6 +565,17 @@
     d_at = lambda t, s: b_out.at[t, :, inner[s]]
     d_ring = Ring(
         z, on_z(1), on_z(3), d_at, d_at, (d_near0, d_near1), (d_pass0, d_pass1), (d_sum0, d_sum1), r_sems.at[3]
+    )
+    u_ring = Ring(
+        z, on_z(1), on_z(3),
+        lambda t, s: dense.at[t, pairs[s], :, third],
+        lambda t, s: grads.at[t, pairs[s], :, third],
+        (u_near0, u_near1), (u_pass0, u_pass1), (u_sum0, u_sum1), r_sems.at[5],
+    )
+    v_at = lambda t, s: u_out.at[t, halves[s]]
+    v_ring = Ring(
+        y, on_y(1), on_y(3), v_at, v_at,
+        (v_near0, v_near1), (v_pass0, v_pass1), (v_sum0, v_sum1), r_sems.at[6],
     )
     e_at = lambda t, s: (d_out if s else c_out).at[pl.ds(pl.multiple_of(t * 8, 8), 8)]
     e_ring = Ring(
@@ -552,8 +597,6 @@
         at = pl.ds(start, stop - start)
         return e_ring.held(x, side)[:, at] + e_ring.sums[side][:, at] + near[:, at]
 
-    halves = (pl.ds(0, 256), pl.ds(256, 256))
-
     def gather_copy(index, view, to):
         return pltpu.make_async_remote_copy(
             src_ref=view, dst_ref=view, send_sem=g_sems.at[0, index],
@@ -566,16 +609,16 @@
             there = lax.rem(4 - step, 4) if back else 0
             at_z, at_y, at_x = (lax.rem(place + there, 4) for place in (z, y, x))
             if number == 0:
-                views = [(gathered.at[z, y, core, at_x], on_x)]
+                views = [(gathered.at[at_x, z, y, core], on_x)]
             elif number == 1:
                 views = [
-                    (gathered.at[z, at_y, core, :, :, halves[0]], on_y),
-                    (gathered.at[at_z, y, core, :, :, halves[1]], on_z),
+                    (gathered.at[:, z, at_y, core, halves[0]], on_y),
+                    (gathered.at[:, at_z, y, core, halves[1]], on_z),
                 ]
             else:
                 views = [
-                    (gathered.at[at_z, :, core, :, :, halves[0]], on_z),
-                    (gathered.at[:, at_y, core, :, :, halves[1]], on_y),
+                    (gathered.at[:, at_z, :, core, halves[0]], on_z),
+                    (gathered.at[:, :, at_y, core, halves[1]], on_y),
                 ]
             for view, axis in views:
                 copies.append(gather_copy(number * 6 + len(copies), view, axis(step)))
@@ -588,11 +631,6 @@
     def arrived(number):
         for copy in stage(number, True):
             copy.wait_recv()
-
-    def pass_on(chunk):
-        table_ring.middle(chunk)
-        if chunk + AHEAD < CHUNKS:
-            table_ring.start(chunk + AHEAD)
 
     rows_chunk = half // CHUNKS
 
@@ -609,78 +647,105 @@
                 grad = mine[rows, :] + table_ring.sums[side][inside, :] + near[inside, :]
                 update(block, grad, store, acc, table_new, acc_new)
 
+    def update_small():
+        @pl.loop(0, TR * RS // 128)
+        def _(block):
+            chip = (block % 8) * 2
+            pieces = gathered.at[block // 8, chip // 4]
+            grad = jnp.concatenate(
+                [pieces[chip % 4 + part // 2, part % 2] for part in range(4)], axis=0
+            )
+            update(block, grad, small, small_acc, small_new, small_acc_new)
+
+    def finish_steps():
+        e_ring.arrive()
+        for side, stop in ((0, CUT), (1, WIDTH - CUT)):
+            total = finish_dense(side, 0, stop)
+            at = pl.ds(side * CUT, stop)
+            for step, before, rows in ((down_step, down_acc, 0), (up_step, up_acc, 4)):
+                grad = total[rows : rows + 4]
+                step[:, at] = grad * lax.rsqrt(before[:, at] + grad * grad)
+
+    u_ring.start()
+    u_ring.start_direct()
+    table_ring.start(0)
+    table_ring.start(1)
+    table_ring.start(2)
+    table_ring.start(3)
+    locals_[2].wait()
+    u_ring.middle()
+    u_ring.finish([u_out.at[pairs[s]] for s in range(2)])
+    v_ring.start()
+    v_ring.start_direct()
     a_ring.start()
     b_ring.start()
-    for chunk in range(AHEAD):
-        table_ring.start(chunk)
-    for copy in locals_[:3]:
-        copy.wait()
-    pass_on(0)
+    v_ring.middle()
+    v_ring.finish([gathered.at[x, z, y, core, halves[s]] for s in range(2)])
+    begin(0)
+    locals_[0].wait()
+    locals_[1].wait()
+    table_ring.middle(0)
+    table_ring.start(4)
+    table_ring.start_direct(0)
     a_ring.middle()
     b_ring.middle()
-    pass_on(1)
-    pass_on(2)
-    pass_on(3)
+    a_ring.start_direct()
+    b_ring.start_direct()
+    table_ring.middle(1)
+    table_ring.start_direct(1)
+    table_ring.start(5)
+    table_ring.middle(2)
+    table_ring.start_direct(2)
+    table_ring.start(6)
+    arrived(0)
+    begin(1)
     for copy in locals_[3:]:
         copy.wait()
+    table_ring.middle(3)
+    table_ring.start_direct(3)
+    table_ring.start(7)
     a_ring.finish([a_out.at[:, :, first[s]] for s in range(2)])
     c_ring.start()
+    c_ring.start_direct()
     b_ring.finish([b_out.at[:, :, inner[s]] for s in range(2)])
     d_ring.start()
+    d_ring.start_direct()
     update_tables(0)
-    pass_on(4)
+    table_ring.middle(4)
+    table_ring.start_direct(4)
+    arrived(1)
+    begin(2)
     c_ring.middle()
     d_ring.middle()
-    update_tables(1)
+    table_ring.middle(5)
+    table_ring.start_direct(5)
     c_ring.finish([c_out.at[:, first[s]] for s in range(2)])
     d_ring.finish([d_out.at[:, inner[s]] for s in range(2)])
     e_ring.start()
-    pass_on(5)
+    e_ring.start_direct()
+    update_tables(1)
+    arrived(2)
+    gather_copy(18, gathered.at[:, :, :, core], partner).start()
+    table_ring.middle(6)
+    table_ring.start_direct(6)
     e_ring.middle()
     update_tables(2)
-    e_ring.arrive()
-    gathered[z, y, core, x] = finish_dense(1, WIDTH - CUT, FULL - CUT)
-    begin(0)
-    pass_on(6)
-    for side, stop in ((0, CUT), (1, WIDTH - CUT)):
-        total = finish_dense(side, 0, stop)
-        at = pl.ds(side * CUT, stop)
-        for step, before, rows in ((down_step, down_acc, 0), (up_step, up_acc, 4)):
-            grad = total[rows : rows + 4]
-            step[:, at] = grad * lax.rsqrt(before[:, at] + grad * grad)
-    arrived(0)
-    begin(1)
+    table_ring.middle(7)
+    table_ring.start_direct(7)
+    gather_copy(18, gathered.at[:, :, :, 1 - core], partner).wait_recv()
+    update_small()
+    finish_steps()
     update_tables(3)
     update_tables(4)
-    arrived(1)
-    begin(2)
-    pass_on(7)
     update_tables(5)
-    arrived(2)
-    gather_copy(18, gathered.at[:, :, core], partner).start()
     update_tables(6)
-    gather_copy(18, gathered.at[:, :, 1 - core], partner).wait_recv()
-
-    @pl.loop(0, TR * RS // 128)
-    def _(block):
-        mixed = gathered.at[block // 8, (block // 2) % 4, block % 2]
-        grad = jnp.concatenate(
-            [
-                mixed[place, :, tile * 128 : (tile + 1) * 128]
-                for place in range(LOCALS)
-                for tile in range(4)
-            ],
-            axis=0,
-        )
-        update(block, grad, small, small_acc, small_new, small_acc_new)
-
     update_tables(7)
-    for ring in (table_ring, a_ring, b_ring, c_ring, d_ring, e_ring):
+    for ring in (table_ring, a_ring, b_ring, c_ring, d_ring, e_ring, u_ring, v_ring):
         ring.drain()
     for number in range(3):
         for copy in stage(number, False):
             copy.wait_send()
-    gather_copy(18, gathered.at[:, :, core], partner).wait_send()
+    gather_copy(18, gathered.at[:, :, :, core], partner).wait_send()
 
 
 def shaped(shape, dtype=F32):
@@ -706,10 +771,10 @@
     send, small, rights, lows = pl.pallas_call(
         dense_kernel,
         out_shape=(
-            shaped((HOSTS, PACK, EMB)), shaped((SAMPLES, TR * EMB)),
+            shaped((HOSTS, PACK, EMB)), shaped((TR, PACK, EMB)),
             shaped((2 * SAMPLES, WIDTH), BF16), shaped((2 * SAMPLES, RANK), BF16),
         ),
-        in_specs=[VMEM] * 3 + [SMEM] * 2 + [VMEM] + [HBM] * 3,
+        in_specs=[VMEM] * 3 + [SMEM] * 2 + [VMEM] * 2 + [HBM] * 3,
         out_specs=(VMEM,) * 4,
         scratch_shapes=[
             pltpu.VMEM((RANK, WIDTH), BF16), pltpu.VMEM((RANK, WIDTH), BF16),
@@ -719,8 +784,7 @@
         name="dense_backward",
     )(
         labels.reshape(1, -1), cross_bias.reshape(-1, 128), head_weight.reshape(-1, 128), head_bias,
-        table_place, bags,
-        features, cross_down, cross_up,
+        table_place, bags, small_ids, features, cross_down, cross_up,
     )
     whole = (RANK, FULL)
     got, ids, dense = pl.pallas_call(
@@ -728,20 +792,20 @@
         out_shape=(
             shaped((HOSTS, PACK, EMB)), shaped((HOSTS * HOT, SAMPLES), jnp.int32), shaped(whole),
         ),
-        in_specs=[HBM] * 4 + [VMEM],
+        in_specs=[HBM] * 4,
         out_specs=(HBM, VMEM, HBM),
         scratch_shapes=[
             pltpu.VMEM((2 * SAMPLES, WIDTH), BF16), pltpu.VMEM((2 * SAMPLES, RANK), BF16),
-            pltpu.VMEM((SAMPLES, TR * EMB), F32), pltpu.VMEM((HOSTS, PACK, EMB), F32),
+            pltpu.VMEM((LOCALS, PACK, EMB), F32), pltpu.VMEM((HOSTS, PACK, EMB), F32),
             pltpu.VMEM((RANK, 2 * SAMPLES), BF16), pltpu.VMEM((RANK, 2 * SAMPLES), BF16),
             pltpu.VMEM(whole, F32), pltpu.VMEM(whole, F32), pltpu.VMEM(whole, F32),
             pltpu.VMEM((TR, SAMPLES, 2 * EMB), BF16),
             pltpu.VMEM((len(TIES), 2, PACK, EMB), F32),
-            DMA((2, HOSTS)), DMA((2, len(TIES))), DMA((2, 4)), DMA((4,)), DMA((3,)), DMA,
+            DMA((2, HOSTS)), DMA((2, len(TIES))), DMA((2, 4)), DMA((2, 4)), DMA((4,)), DMA((3,)), DMA,
         ],
         compiler_params=params(60, collective_id=0, has_side_effects=True),
         name="exchange",
-    )(send, rights, lows, small, small_ids)
+    )(send, rights, lows, small)
     tables = pl.pallas_call(
         pooled_kernel,
         out_shape=shaped((LOCALS * SHARD, EMB)),
@@ -758,7 +822,7 @@
         near = [pltpu.VMEM(second_shape, F32), pltpu.VMEM(first_shape, F32)]
         return near + [pltpu.VMEM(first_shape, F32), pltpu.VMEM(second_shape, F32)] * 2
 
-    rest = FULL - CUT
+    rest = WIDTH - CUT
     half = SHARD // 2
     table_new, acc_new, small_new, small_acc_new, down_step, up_step = pl.pallas_call(
         reduce_kernel,
@@ -771,22 +835,25 @@
         out_specs=(VMEM,) * 6,
         scratch_shapes=[
             pltpu.VMEM((SHARD, EMB), F32), pltpu.VMEM((TR * RS, EMB), F32),
-            pltpu.VMEM((4, 4, 2, LOCALS, 8, TR * EMB), F32), pltpu.VMEM((SHARD, EMB), F32),
+            pltpu.VMEM((LOCALS, 4, 4, 2, 32, EMB), F32), pltpu.VMEM((SHARD, EMB), F32),
             pltpu.VMEM((half, EMB), F32), pltpu.VMEM((half, EMB), F32),
             pltpu.VMEM((4, 4, 32, FULL), F32),
         ]
         + ring_buffers((half, EMB), (half, EMB))
-        + ring_buffers((4, 32, 1024), (4, 32, 1024))
-        + ring_buffers((4, 32, 1024), (4, 32, 896))
-        + ring_buffers((32, 1024), (32, 1024))
-        + ring_buffers((32, 1024), (32, 896))
+        + ring_buffers((4, 32, 896), (4, 32, 896))
+        + ring_buffers((4, 32, 896), (4, 32, 768))
+        + ring_buffers((32, 896), (32, 896))
+        + ring_buffers((32, 896), (32, 768))
         + ring_buffers((8, CUT), (8, rest))
+        + ring_buffers((2, 32, EMB), (2, 32, EMB))
+        + ring_buffers((16, EMB), (16, EMB))
         + [
             pltpu.VMEM((4, 32, CUT), F32), pltpu.VMEM((4, 32, rest), F32),
             pltpu.VMEM((32, CUT), F32), pltpu.VMEM((32, rest), F32),
-            DMA((2, 6 * CHUNKS)), DMA((5, 2, 6)), DMA((2, 19)), DMA((6,)),
+            pltpu.VMEM((4, 32, EMB), F32),
+            DMA((2, 6 * CHUNKS)), DMA((7, 2, 6)), DMA((2, 19)), DMA((6,)),
         ],
-        compiler_params=params(40, collective_id=1, has_side_effects=True),
+        compiler_params=params(48, collective_id=1, has_side_effects=True),
         name="reduce_update",
     )(
         tables.reshape(LOCALS, SHARD, EMB), dense.reshape(4, 4, 32, FULL), table_store, small_store,

time: 182 us -> 175 us (0.962)
  Pallas kernels: 170 us -> 166 us
    pallas_call x1, Pallas kernels: 93.2 us -> 87.7 us  [on_device(): pl.pallas_call(reduce_kernel, out_shape=(shaped((SHARD, EMB)), shaped((SH...]
    unnamed x18 -> x14, local copies, waits for them, and re-layouts: 6.71 us -> 5.12 us
where the time goes in v4:
time: 175 us; the launch traced here: 173 us
  Pallas kernels  166 us (95%)
  local copies, waits for them, and re-layouts  5.12 us (3%)
    pallas_call x1, Pallas kernels, on_device(): pl.pallas_call(reduce_kernel, out_shape=(shaped((SHARD, EMB)), shaped((SH...  87.7 us
    pallas_call x1, Pallas kernels, on_device(): pl.pallas_call(exchange_kernel, out_shape=(shaped((HOSTS, PACK, EMB)), sh...  39.4 us
    pallas_call x1, Pallas kernels, on_device(): pl.pallas_call(pooled_kernel, out_shape=shaped((LOCALS * SHARD, EMB)), in...  29.9 us
    pallas_call x1, Pallas kernels, on_device(): pl.pallas_call(dense_kernel, out_shape=(shaped((HOSTS, PACK, EMB)), shape...  9.23 us
    unnamed x14, local copies, waits for them, and re-layouts  5.12 us

profile of v4, /device:TPU:0, one launch (start us, length us, event | category | flops | bytes accessed | tf_op | source)
XLA Modules:
  0.0 172.6 jit_solution(9560465536688853702)
XLA Ops:
  1.3 9.2 %dense_backward.1 = (f32[32,136,128]{2,1,0:T(8,128)}, f32[4,136,128]{2,1,0:T(8,128)}, bf16[256,3456]{1,0:T(8,128)(2,1)}, bf16[256,512]{1,0:T(8,128)(2,1)}) custom-call(s32[1,128]{1,0:T(1,128)} %bitcast.23, f32[27,128]{1,0:T(8,128)} %bitcast.20, f32[27,128]{1,0:T(8,128)} %bitcast.21, f32[1]{0:T(128)S(6)} %copy.28.head_bias, s32[22]{0:T(128)} %place.1, ...), custom_call_target="tpu_custom_call" | custom-call | tf_op jit(solution)/shard_map/dense_backward/pallas_call | solution.py:771
  10.5 39.4 %exchange.1 = (f32[32,136,128]{2,1,0:T(8,128)}, s32[128,128]{1,0:T(8,128)}, f32[512,3584]{1,0:T(8,128)}) custom-call(f32[32,136,128]{2,1,0:T(8,128)} %get-tuple-element.19.send, bf16[256,3456]{1,0:T(8,128)(2,1)} %get-tuple-element.20.rights_hbm, bf16[256,512]{1,0:T(8,128)(2,1)} %get-tuple-element.21.lows_hbm, f32[4,136,128]{2,1,0:T(8,128)} %get-tuple-element.22.small_hbm), custom_call_target="tpu_custom_call" | custom-call | tf_op jit(solution)/shard_map/exchange/pallas_call | solution.py:790
  49.9 0.0 copy-start
  49.9 0.0 copy-start.1
  49.9 0.0 copy-start.2
  49.9 0.0 copy-start.3
  49.9 29.9 %pooled_rows.1 = f32[16384,128]{1,0:T(8,128)} custom-call(s32[16384]{0:T(1024)} %bitcast.18, f32[32,136,128]{2,1,0:T(8,128)} %get-tuple-element.24.grads_hbm), custom_call_target="tpu_custom_call" | custom-call | tf_op jit(solution)/shard_map/pooled_rows/pallas_call | solution.py:809
  79.8 0.0 copy-done
  79.8 0.0 copy-done.1
  79.8 0.0 copy-done.2
  79.8 0.0 copy-done.3
  79.8 87.7 %reduce_update.1 = (f32[4096,128]{1,0:T(8,128)S(1)}, f32[32,128]{1,0:T(8,128)S(1)}, f32[4096,128]{1,0:T(8,128)S(1)}, f32[32,128]{1,0:T(8,128)S(1)}, f32[4,3456]{1,0:T(4,128)S(1)}, /*index=5*/f32[4,3456]{1,0:T(4,128)S(1)}) custom-call(f32[4,4096,128]{2,1,0:T(8,128)} %bitcast.16, f32[4,4,32,3584]{3,2,1,0:T(8,128)} %bitcast.17, f32[4096,128]{1,0:T(8,128)} %store_hbm.1, ...), custom_call_target="tpu_custom_call" | custom-call | tf_op jit(solution)/shard_map/reduce_update/pallas_call | solution.py:827
  167.5 1.3 copy.29
  168.8 0.6 copy.30
  169.4 1.3 copy.31
  170.7 0.6 copy.32
  171.4 0.6 copy.33
  172.0 0.6 copy.34
Async XLA Ops:
  49.9 29.9 %copy-start = (f32[4,3456]{1,0:T(4,128)S(1)}, f32[4,3456]{1,0:T(4,128)}, u32[]{:S(2)}) copy-start(f32[4,3456]{1,0:T(4,128)} %down_acc.1) | copy-start | bytes 165892
  49.9 29.9 %copy-start.1 = (f32[4,3456]{1,0:T(4,128)S(1)}, f32[4,3456]{1,0:T(4,128)}, u32[]{:S(2)}) copy-start(f32[4,3456]{1,0:T(4,128)} %up_acc.1) | copy-start | bytes 165892
  49.9 29.9 %copy-start.2 = (f32[4096]{0:T(1024)S(1)}, f32[4096]{0:T(1024)}, u32[]{:S(2)}) copy-start(f32[4096]{0:T(1024)} %param.27) | copy-start | bytes 49156
  49.9 29.9 %copy-start.3 = (f32[4096]{0:T(1024)S(1)}, f32[4096]{0:T(1024)}, u32[]{:S(2)}) copy-start(f32[4096]{0:T(1024)} %param.29) | copy-start | bytes 49156

commit v5 on v4

--- a/solution.py
+++ b/solution.py
@@ -41,9 +41,9 @@
     )
 
 
-def dense_kernel(
+def dense_backward(
     labels, bias, head, head_bias, place, bags, small_ids, features_hbm, down_hbm, up_hbm,
-    send, small, rights, lows, down, up, cross, sems,
+    pieces, send, small, rights, lows, down, up, cross, sems,
 ):
     features = rights.at[0:SAMPLES]
     features_copy = pltpu.make_async_copy(features_hbm, features, sems.at[2])
@@ -53,9 +53,11 @@
     down_copy.start()
     up_copy.start()
 
-    @pl.loop(0, HOSTS)
-    def _(slot):
-        send[slot] = jnp.zeros((PACK, EMB), F32)
+    @pl.loop(0, TS)
+    def _(table):
+        pieces[table, pl.ds(SAMPLES, 8), :] = jnp.concatenate(
+            [bags[table].astype(F32), jnp.zeros((HOT, EMB), F32)], axis=0
+        )
 
     for table in range(TR):
         small[table, SAMPLES:, :] = jnp.zeros((PACK - SAMPLES, EMB), F32)
@@ -100,32 +102,31 @@
             piece = grad[:, tile * 128 : (tile + 1) * 128]
             table = start // 128 + tile - 1
             if 0 <= table < TS:
-                slot = place[table]
-                send[slot, 0:SAMPLES, :] = piece
-                send[slot, SAMPLES : SAMPLES + HOT, :] = bags[table].astype(F32)
+                pieces[table, 0:SAMPLES, :] = piece
             elif table >= TS:
                 small[table - TS, 0:SAMPLES, :] = piece
 
+    @pl.loop(0, HOSTS)
+    def _(slot):
+        held = jnp.int32(-1)
+        for table in range(TS):
+            held = jnp.where(place[table] == slot, table, held)
+        keep = jnp.where(held >= 0, 1, 0)
+        send[slot] = jnp.where(keep == 1, pieces[jnp.maximum(held, 0)], 0.0)
+
 
 def exchange_kernel(
-    send, rights_hbm, lows_hbm, small_hbm,
+    labels, bias, head, head_bias, place, bags, small_ids, features_hbm, down_hbm, up_hbm,
     got_hbm, ids, dense,
+    pieces, send, small_mine, down, up, cross, dense_sems,
     rights, lows, small, got, left_own, left_other, own, other, arrived, split, relayed,
-    sems, relay_sems, core_sems, small_sems, out_sems, in_sems, own_sem,
+    sems, relay_sems, core_sems, small_sems, out_sems, in_sem, own_sem,
 ):
     host = lax.axis_index("hst")
     core = lax.rem(host, 2)
     z, y = host // 8, (host // 2) % 4
     x = lax.axis_index("local")
     partner = host + 1 - 2 * core
-    operands = [
-        pltpu.make_async_copy(source, target, in_sems.at[i])
-        for i, (source, target) in enumerate(
-            ((lows_hbm, lows), (rights_hbm, rights), (small_hbm.at[x], small.at[x]))
-        )
-    ]
-    for copy in operands:
-        copy.start()
     barrier = pltpu.get_barrier_semaphore()
 
     @pl.loop(1, HOSTS)
@@ -204,7 +205,7 @@
     def small_copy(step, slot):
         to = lax.rem(x + step, 4)
         return pltpu.make_async_remote_copy(
-            src_ref=small_hbm.at[to],
+            src_ref=small_mine.at[to],
             dst_ref=small.at[slot],
             send_sem=small_sems.at[0, step],
             recv_sem=small_sems.at[1, step],
@@ -212,6 +213,12 @@
             device_id_type=MESH,
         )
 
+    dense_backward(
+        labels, bias, head, head_bias, place, bags, small_ids, features_hbm, down_hbm, up_hbm,
+        pieces, send, small_mine, rights, lows, down, up, cross, dense_sems,
+    )
+    small_own = pltpu.make_async_copy(small_mine.at[x], small.at[x], in_sem)
+    small_own.start()
     pl.semaphore_wait(barrier, HOSTS + 2)
     for step in (1, 2, 3):
         small_copy(step, x).start()
@@ -244,8 +251,7 @@
                 left[group * 128 : (group + 1) * 128, :], rights[:, at]
             )
 
-    for copy in operands:
-        copy.wait()
+    small_own.wait()
     for step in (1, 2, 3):
         small_copy(step, lax.rem(x - step + 4, 4)).wait_recv()
 
@@ -768,44 +774,33 @@
 ):
     bags = jnp.transpose(bag_rows, (1, 2, 0))
     small_ids = jnp.transpose(small_rows, (1, 2, 0))
-    send, small, rights, lows = pl.pallas_call(
-        dense_kernel,
-        out_shape=(
-            shaped((HOSTS, PACK, EMB)), shaped((TR, PACK, EMB)),
-            shaped((2 * SAMPLES, WIDTH), BF16), shaped((2 * SAMPLES, RANK), BF16),
-        ),
-        in_specs=[VMEM] * 3 + [SMEM] * 2 + [VMEM] * 2 + [HBM] * 3,
-        out_specs=(VMEM,) * 4,
-        scratch_shapes=[
-            pltpu.VMEM((RANK, WIDTH), BF16), pltpu.VMEM((RANK, WIDTH), BF16),
-            pltpu.VMEM((SAMPLES, WIDTH), F32), DMA((3,)),
-        ],
-        compiler_params=params(60),
-        name="dense_backward",
-    )(
-        labels.reshape(1, -1), cross_bias.reshape(-1, 128), head_weight.reshape(-1, 128), head_bias,
-        table_place, bags, small_ids, features, cross_down, cross_up,
-    )
     whole = (RANK, FULL)
     got, ids, dense = pl.pallas_call(
         exchange_kernel,
         out_shape=(
             shaped((HOSTS, PACK, EMB)), shaped((HOSTS * HOT, SAMPLES), jnp.int32), shaped(whole),
         ),
-        in_specs=[HBM] * 4,
+        in_specs=[VMEM] * 3 + [SMEM] * 2 + [VMEM] * 2 + [HBM] * 3,
         out_specs=(HBM, VMEM, HBM),
         scratch_shapes=[
+            pltpu.VMEM((TS, PACK, EMB), F32), pltpu.VMEM((HOSTS, PACK, EMB), F32),
+            pltpu.VMEM((TR, PACK, EMB), F32),
+            pltpu.VMEM((RANK, WIDTH), BF16), pltpu.VMEM((RANK, WIDTH), BF16),
+            pltpu.VMEM((SAMPLES, WIDTH), F32), DMA((3,)),
             pltpu.VMEM((2 * SAMPLES, WIDTH), BF16), pltpu.VMEM((2 * SAMPLES, RANK), BF16),
             pltpu.VMEM((LOCALS, PACK, EMB), F32), pltpu.VMEM((HOSTS, PACK, EMB), F32),
             pltpu.VMEM((RANK, 2 * SAMPLES), BF16), pltpu.VMEM((RANK, 2 * SAMPLES), BF16),
             pltpu.VMEM(whole, F32), pltpu.VMEM(whole, F32), pltpu.VMEM(whole, F32),
             pltpu.VMEM((TR, SAMPLES, 2 * EMB), BF16),
             pltpu.VMEM((len(TIES), 2, PACK, EMB), F32),
-            DMA((2, HOSTS)), DMA((2, len(TIES))), DMA((2, 4)), DMA((2, 4)), DMA((4,)), DMA((3,)), DMA,
+            DMA((2, HOSTS)), DMA((2, len(TIES))), DMA((2, 4)), DMA((2, 4)), DMA((4,)), DMA, DMA,
         ],
         compiler_params=params(60, collective_id=0, has_side_effects=True),
-        name="exchange",
-    )(send, rights, lows, small)
+        name="dense_exchange",
+    )(
+        labels.reshape(1, -1), cross_bias.reshape(-1, 128), head_weight.reshape(-1, 128), head_bias,
+        table_place, bags, small_ids, features, cross_down, cross_up,
+    )
     tables = pl.pallas_call(
         pooled_kernel,
         out_shape=shaped((LOCALS * SHARD, EMB)),

time: 175 us -> 168 us (0.960); the launches traced: 173 us -> 168 us
  Pallas kernels: 166 us -> 161 us
    pallas_call x1 -> x0, Pallas kernels: 9.23 us -> none  [on_device(): pl.pallas_call(dense_kernel, out_shape=(shaped((HOSTS, PACK, EMB)), shape...]
    pallas_call x1, Pallas kernels: 39.4 us -> 43.2 us  [on_device(): pl.pallas_call(exchange_kernel, out_shape=(shaped((HOSTS, PACK, EMB)), sh...]
where the time goes in v5:
time: 168 us
  Pallas kernels  161 us (96%)
  local copies, waits for them, and re-layouts  5.12 us (3%)
    pallas_call x1, Pallas kernels, on_device(): pl.pallas_call(reduce_kernel, out_shape=(shaped((SHARD, EMB)), shaped((SH...  88.3 us
    pallas_call x1, Pallas kernels, on_device(): pl.pallas_call(exchange_kernel, out_shape=(shaped((HOSTS, PACK, EMB)), sh...  43.2 us
    pallas_call x1, Pallas kernels, on_device(): pl.pallas_call(pooled_kernel, out_shape=shaped((LOCALS * SHARD, EMB)), in...  29.9 us
    unnamed x14, local copies, waits for them, and re-layouts  5.12 us

profile of v5, /device:TPU:0, one launch (start us, length us, event | category | flops | bytes accessed | tf_op | source)
XLA Modules:
  0.0 167.9 jit_solution(8374817132436950018)
XLA Ops:
  1.3 43.2 %dense_exchange.1 = (f32[32,136,128]{2,1,0:T(8,128)}, s32[128,128]{1,0:T(8,128)}, f32[512,3584]{1,0:T(8,128)}) custom-call(s32[1,128]{1,0:T(1,128)} %bitcast.23, f32[27,128]{1,0:T(8,128)} %bitcast.20, f32[27,128]{1,0:T(8,128)} %bitcast.21, f32[1]{0:T(128)S(6)} %copy.28.head_bias, s32[22]{0:T(128)} %place.1, s32[22,4,128]{2,1,0:T(4,128)} %bitcast.19, ...), custom_call_target="tpu_custom_call" | custom-call | tf_op jit(solution)/shard_map/dense_exchange/pallas_call | solution.py:778
  44.5 0.0 copy-start
  44.5 0.0 copy-start.1
  44.5 0.0 copy-start.2
  44.5 0.0 copy-start.3
  44.5 29.9 %pooled_rows.1 = f32[16384,128]{1,0:T(8,128)} custom-call(s32[16384]{0:T(1024)} %bitcast.18, f32[32,136,128]{2,1,0:T(8,128)} %get-tuple-element.16.grads_hbm), custom_call_target="tpu_custom_call" | custom-call | tf_op jit(solution)/shard_map/pooled_rows/pallas_call | solution.py:804
  74.4 0.0 copy-done
  74.4 0.0 copy-done.1
  74.4 0.0 copy-done.2
  74.5 0.0 copy-done.3
  74.5 88.3 %reduce_update.1 = (f32[4096,128]{1,0:T(8,128)S(1)}, f32[32,128]{1,0:T(8,128)S(1)}, f32[4096,128]{1,0:T(8,128)S(1)}, f32[32,128]{1,0:T(8,128)S(1)}, f32[4,3456]{1,0:T(4,128)S(1)}, /*index=5*/f32[4,3456]{1,0:T(4,128)S(1)}) custom-call(f32[4,4096,128]{2,1,0:T(8,128)} %bitcast.16, f32[4,4,32,3584]{3,2,1,0:T(8,128)} %bitcast.17, f32[4096,128]{1,0:T(8,128)} %store_hbm.1, ...), custom_call_target="tpu_custom_call" | custom-call | tf_op jit(solution)/shard_map/reduce_update/pallas_call | solution.py:822
  162.8 1.3 copy.29
  164.1 0.6 copy.30
  164.7 1.3 copy.31
  166.0 0.6 copy.32
  166.7 0.6 copy.33
  167.3 0.6 copy.34
Async XLA Ops:
  44.5 29.9 %copy-start = (f32[4,3456]{1,0:T(4,128)S(1)}, f32[4,3456]{1,0:T(4,128)}, u32[]{:S(2)}) copy-start(f32[4,3456]{1,0:T(4,128)} %down_acc.1) | copy-start | bytes 165892
  44.5 29.9 %copy-start.1 = (f32[4,3456]{1,0:T(4,128)S(1)}, f32[4,3456]{1,0:T(4,128)}, u32[]{:S(2)}) copy-start(f32[4,3456]{1,0:T(4,128)} %up_acc.1) | copy-start | bytes 165892
  44.5 29.9 %copy-start.2 = (f32[4096]{0:T(1024)S(1)}, f32[4096]{0:T(1024)}, u32[]{:S(2)}) copy-start(f32[4096]{0:T(1024)} %param.27) | copy-start | bytes 49156
  44.5 29.9 %copy-start.3 = (f32[4096]{0:T(1024)S(1)}, f32[4096]{0:T(1024)}, u32[]{:S(2)}) copy-start(f32[4096]{0:T(1024)} %param.29) | copy-start | bytes 49156

commit v6 on v5

--- a/solution.py
+++ b/solution.py
@@ -674,10 +674,8 @@
 
     u_ring.start()
     u_ring.start_direct()
-    table_ring.start(0)
-    table_ring.start(1)
-    table_ring.start(2)
-    table_ring.start(3)
+    for chunk in range(CHUNKS):
+        table_ring.start(chunk)
     locals_[2].wait()
     u_ring.middle()
     u_ring.finish([u_out.at[pairs[s]] for s in range(2)])
@@ -691,7 +689,6 @@
     locals_[0].wait()
     locals_[1].wait()
     table_ring.middle(0)
-    table_ring.start(4)
     table_ring.start_direct(0)
     a_ring.middle()
     b_ring.middle()
@@ -699,17 +696,14 @@
     b_ring.start_direct()
     table_ring.middle(1)
     table_ring.start_direct(1)
-    table_ring.start(5)
     table_ring.middle(2)
     table_ring.start_direct(2)
-    table_ring.start(6)
     arrived(0)
     begin(1)
     for copy in locals_[3:]:
         copy.wait()
     table_ring.middle(3)
     table_ring.start_direct(3)
-    table_ring.start(7)
     a_ring.finish([a_out.at[:, :, first[s]] for s in range(2)])
     c_ring.start()
     c_ring.start_direct()
@@ -741,11 +735,8 @@
     gather_copy(18, gathered.at[:, :, :, 1 - core], partner).wait_recv()
     update_small()
     finish_steps()
-    update_tables(3)
-    update_tables(4)
-    update_tables(5)
-    update_tables(6)
-    update_tables(7)
+    for chunk in range(3, CHUNKS):
+        update_tables(chunk)
     for ring in (table_ring, a_ring, b_ring, c_ring, d_ring, e_ring, u_ring, v_ring):
         ring.drain()
     for number in range(3):

time: 168 us -> 164 us (0.976)
  Pallas kernels: 161 us -> 157 us
    pallas_call x1, Pallas kernels: 88.3 us -> 84 us  [on_device(): pl.pallas_call(reduce_kernel, out_shape=(shaped((SHARD, EMB)), shaped((SH...]
where the time goes in v6:
time: 164 us
  Pallas kernels  157 us (96%)
  local copies, waits for them, and re-layouts  5.12 us (3%)
    pallas_call x1, Pallas kernels, on_device(): pl.pallas_call(reduce_kernel, out_shape=(shaped((SHARD, EMB)), shaped((SH...  84 us
    pallas_call x1, Pallas kernels, on_device(): pl.pallas_call(exchange_kernel, out_shape=(shaped((HOSTS, PACK, EMB)), sh...  43.2 us
    pallas_call x1, Pallas kernels, on_device(): pl.pallas_call(pooled_kernel, out_shape=shaped((LOCALS * SHARD, EMB)), in...  29.9 us
    unnamed x14, local copies, waits for them, and re-layouts  5.12 us

profile of v6, /device:TPU:0, one launch (start us, length us, event | category | flops | bytes accessed | tf_op | source)
XLA Modules:
  0.0 163.6 jit_solution(3285139749016840226)
XLA Ops:
  1.3 43.2 %dense_exchange.1 = (f32[32,136,128]{2,1,0:T(8,128)}, s32[128,128]{1,0:T(8,128)}, f32[512,3584]{1,0:T(8,128)}) custom-call(s32[1,128]{1,0:T(1,128)} %bitcast.23, f32[27,128]{1,0:T(8,128)} %bitcast.20, f32[27,128]{1,0:T(8,128)} %bitcast.21, f32[1]{0:T(128)S(6)} %copy.28.head_bias, s32[22]{0:T(128)} %place.1, s32[22,4,128]{2,1,0:T(4,128)} %bitcast.19, ...), custom_call_target="tpu_custom_call" | custom-call | tf_op jit(solution)/shard_map/dense_exchange/pallas_call | solution.py:769
  44.5 0.0 copy-start
  44.5 0.0 copy-start.1
  44.5 0.0 copy-start.2
  44.5 0.0 copy-start.3
  44.5 29.9 %pooled_rows.1 = f32[16384,128]{1,0:T(8,128)} custom-call(s32[16384]{0:T(1024)} %bitcast.18, f32[32,136,128]{2,1,0:T(8,128)} %get-tuple-element.16.grads_hbm), custom_call_target="tpu_custom_call" | custom-call | tf_op jit(solution)/shard_map/pooled_rows/pallas_call | solution.py:795
  74.4 0.0 copy-done
  74.4 0.0 copy-done.1
  74.4 0.0 copy-done.2
  74.5 0.0 copy-done.3
  74.5 84.0 %reduce_update.1 = (f32[4096,128]{1,0:T(8,128)S(1)}, f32[32,128]{1,0:T(8,128)S(1)}, f32[4096,128]{1,0:T(8,128)S(1)}, f32[32,128]{1,0:T(8,128)S(1)}, f32[4,3456]{1,0:T(4,128)S(1)}, /*index=5*/f32[4,3456]{1,0:T(4,128)S(1)}) custom-call(f32[4,4096,128]{2,1,0:T(8,128)} %bitcast.16, f32[4,4,32,3584]{3,2,1,0:T(8,128)} %bitcast.17, f32[4096,128]{1,0:T(8,128)} %store_hbm.1, ...), custom_call_target="tpu_custom_call" | custom-call | tf_op jit(solution)/shard_map/reduce_update/pallas_call | solution.py:813
  158.5 1.3 copy.29
  159.8 0.6 copy.30
  160.4 1.3 copy.31
  161.7 0.6 copy.32
  162.3 0.6 copy.33
  163.0 0.6 copy.34
Async XLA Ops:
  44.5 29.9 %copy-start = (f32[4,3456]{1,0:T(4,128)S(1)}, f32[4,3456]{1,0:T(4,128)}, u32[]{:S(2)}) copy-start(f32[4,3456]{1,0:T(4,128)} %down_acc.1) | copy-start | bytes 165892
  44.5 29.9 %copy-start.1 = (f32[4,3456]{1,0:T(4,128)S(1)}, f32[4,3456]{1,0:T(4,128)}, u32[]{:S(2)}) copy-start(f32[4,3456]{1,0:T(4,128)} %up_acc.1) | copy-start | bytes 165892
  44.5 29.9 %copy-start.2 = (f32[4096]{0:T(1024)S(1)}, f32[4096]{0:T(1024)}, u32[]{:S(2)}) copy-start(f32[4096]{0:T(1024)} %param.27) | copy-start | bytes 49156
  44.5 29.9 %copy-start.3 = (f32[4096]{0:T(1024)S(1)}, f32[4096]{0:T(1024)}, u32[]{:S(2)}) copy-start(f32[4096]{0:T(1024)} %param.29) | copy-start | bytes 49156

commit v7 on v6

--- a/solution.py
+++ b/solution.py
@@ -531,12 +531,19 @@
     locals_ = [
         pltpu.make_async_copy(tables.at[right, pl.ds(0, half)], ahead, local_sems.at[0]),
         pltpu.make_async_copy(tables.at[left, pl.ds(half, half)], behind, local_sems.at[1]),
-        pltpu.make_async_copy(dense, grads, local_sems.at[2]),
+        pltpu.make_async_copy(
+            dense.at[:, :, :, pl.ds(WIDTH, EMB)], grads.at[:, :, :, pl.ds(WIDTH, EMB)],
+            local_sems.at[2],
+        ),
         pltpu.make_async_copy(tables.at[x], mine, local_sems.at[3]),
         pltpu.make_async_copy(store_hbm, store, local_sems.at[4]),
         pltpu.make_async_copy(small_hbm, small, local_sems.at[5]),
+        pltpu.make_async_copy(
+            dense.at[:, :, :, pl.ds(0, WIDTH)], grads.at[:, :, :, pl.ds(0, WIDTH)],
+            local_sems.at[6],
+        ),
     ]
-    for copy in locals_:
+    for copy in (locals_[2], locals_[0], locals_[1], locals_[6]):
         copy.start()
     pl.semaphore_wait(barrier, 10)
 
@@ -677,6 +684,8 @@
     for chunk in range(CHUNKS):
         table_ring.start(chunk)
     locals_[2].wait()
+    for copy in locals_[3:6]:
+        copy.start()
     u_ring.middle()
     u_ring.finish([u_out.at[pairs[s]] for s in range(2)])
     v_ring.start()
@@ -688,6 +697,7 @@
     begin(0)
     locals_[0].wait()
     locals_[1].wait()
+    locals_[6].wait()
     table_ring.middle(0)
     table_ring.start_direct(0)
     a_ring.middle()
@@ -700,7 +710,7 @@
     table_ring.start_direct(2)
     arrived(0)
     begin(1)
-    for copy in locals_[3:]:
+    for copy in locals_[3:6]:
         copy.wait()
     table_ring.middle(3)
     table_ring.start_direct(3)
@@ -837,7 +847,7 @@
             pltpu.VMEM((4, 32, CUT), F32), pltpu.VMEM((4, 32, rest), F32),
             pltpu.VMEM((32, CUT), F32), pltpu.VMEM((32, rest), F32),
             pltpu.VMEM((4, 32, EMB), F32),
-            DMA((2, 6 * CHUNKS)), DMA((7, 2, 6)), DMA((2, 19)), DMA((6,)),
+            DMA((2, 6 * CHUNKS)), DMA((7, 2, 6)), DMA((2, 19)), DMA((7,)),
         ],
         compiler_params=params(48, collective_id=1, has_side_effects=True),
         name="reduce_update",

time: 164 us -> 165 us (level)
  no operation moved by 1% of the time
where the time goes in v7:
time: 165 us
  Pallas kernels  158 us (96%)
  local copies, waits for them, and re-layouts  5.12 us (3%)
    pallas_call x1, Pallas kernels, on_device(): pl.pallas_call(reduce_kernel, out_shape=(shaped((SHARD, EMB)), shaped((SH...  85 us
    pallas_call x1, Pallas kernels, on_device(): pl.pallas_call(exchange_kernel, out_shape=(shaped((HOSTS, PACK, EMB)), sh...  43.2 us
    pallas_call x1, Pallas kernels, on_device(): pl.pallas_call(pooled_kernel, out_shape=shaped((LOCALS * SHARD, EMB)), in...  29.9 us
    unnamed x14, local copies, waits for them, and re-layouts  5.12 us

profile of v7, /device:TPU:0, one launch (start us, length us, event | category | flops | bytes accessed | tf_op | source)
XLA Modules:
  0.0 164.5 jit_solution(915287641015449805)
XLA Ops:
  1.3 43.2 %dense_exchange.1 = (f32[32,136,128]{2,1,0:T(8,128)}, s32[128,128]{1,0:T(8,128)}, f32[512,3584]{1,0:T(8,128)}) custom-call(s32[1,128]{1,0:T(1,128)} %bitcast.23, f32[27,128]{1,0:T(8,128)} %bitcast.20, f32[27,128]{1,0:T(8,128)} %bitcast.21, f32[1]{0:T(128)S(6)} %copy.28.head_bias, s32[22]{0:T(128)} %place.1, s32[22,4,128]{2,1,0:T(4,128)} %bitcast.19, ...), custom_call_target="tpu_custom_call" | custom-call | tf_op jit(solution)/shard_map/dense_exchange/pallas_call | solution.py:779
  44.5 0.0 copy-start
  44.5 0.0 copy-start.1
  44.5 0.0 copy-start.2
  44.5 0.0 copy-start.3
  44.5 29.9 %pooled_rows.1 = f32[16384,128]{1,0:T(8,128)} custom-call(s32[16384]{0:T(1024)} %bitcast.18, f32[32,136,128]{2,1,0:T(8,128)} %get-tuple-element.16.grads_hbm), custom_call_target="tpu_custom_call" | custom-call | tf_op jit(solution)/shard_map/pooled_rows/pallas_call | solution.py:805
  74.4 0.0 copy-done
  74.4 0.0 copy-done.1
  74.4 0.0 copy-done.2
  74.5 0.0 copy-done.3
  74.5 85.0 %reduce_update.1 = (f32[4096,128]{1,0:T(8,128)S(1)}, f32[32,128]{1,0:T(8,128)S(1)}, f32[4096,128]{1,0:T(8,128)S(1)}, f32[32,128]{1,0:T(8,128)S(1)}, f32[4,3456]{1,0:T(4,128)S(1)}, /*index=5*/f32[4,3456]{1,0:T(4,128)S(1)}) custom-call(f32[4,4096,128]{2,1,0:T(8,128)} %bitcast.16, f32[4,4,32,3584]{3,2,1,0:T(8,128)} %bitcast.17, f32[4096,128]{1,0:T(8,128)} %store_hbm.1, ...), custom_call_target="tpu_custom_call" | custom-call | tf_op jit(solution)/shard_map/reduce_update/pallas_call | solution.py:823
  159.5 1.3 copy.29
  160.8 0.6 copy.30
  161.4 1.3 copy.31
  162.7 0.6 copy.32
  163.3 0.6 copy.33
  163.9 0.6 copy.34
Async XLA Ops:
  44.5 29.9 %copy-start = (f32[4,3456]{1,0:T(4,128)S(1)}, f32[4,3456]{1,0:T(4,128)}, u32[]{:S(2)}) copy-start(f32[4,3456]{1,0:T(4,128)} %down_acc.1) | copy-start | bytes 165892
  44.5 29.9 %copy-start.1 = (f32[4,3456]{1,0:T(4,128)S(1)}, f32[4,3456]{1,0:T(4,128)}, u32[]{:S(2)}) copy-start(f32[4,3456]{1,0:T(4,128)} %up_acc.1) | copy-start | bytes 165892
  44.5 29.9 %copy-start.2 = (f32[4096]{0:T(1024)S(1)}, f32[4096]{0:T(1024)}, u32[]{:S(2)}) copy-start(f32[4096]{0:T(1024)} %param.27) | copy-start | bytes 49156
  44.5 29.9 %copy-start.3 = (f32[4096]{0:T(1024)S(1)}, f32[4096]{0:T(1024)}, u32[]{:S(2)}) copy-start(f32[4096]{0:T(1024)} %param.29) | copy-start | bytes 49156
